TPU v7x, 256 devices: a whole 4x4x8 slice. The times are simulated.
256 devices in a mesh: ctx: 32 (over z, x), head: 8 (over y, core).
Axes of the slice: x: 4, y: 4, z: 8, core: 2. Of those that a mesh axis runs over, the one named last changes fastest.
Arguments:
- state_query: bfloat16 [16384, 4096], P('ctx', 'head'), may hold values from -6 to 6
- state_key: bfloat16 [16384, 4096], P('ctx', 'head'), may hold values from -0.5 to 0.5
- state_value: bfloat16 [16384, 4096], P('ctx', 'head'), may hold values from -6 to 6
- state_gate: bfloat16 [16384, 4096], P('ctx', 'head'), may hold values from -40 to 40
- log_decay: float32 [32, 16384], P('head', 'ctx'), may hold values from -2.5 to 0
- level_gate: float32 [32, 20, 16384], P('head', None, 'ctx'), may hold values from 0.2 to 2
- norm_gain: float32 [4096], P('head'), may hold values from 0.1 to 1.9
- attention_query: bfloat16 [16384, 4096], P('ctx', 'head'), may hold values from -170 to 170
- attention_key: bfloat16 [16384, 4096], P('ctx', 'head'), may hold values from -6.5 to 6.5
- attention_value: bfloat16 [16384, 4096], P('ctx', 'head'), may hold values from -6 to 6
Outputs:
- mixer_output: bfloat16 [16384, 4096], P('ctx', 'head')
- attention_output: bfloat16 [16384, 4096], P('ctx', 'head')
All inputs are finite; a program needn't handle non-finite values.
Results may differ from a plain program's by a relative error of at most 0.0062.
Values may be sent and summed in bfloat16 or wider, within the bound.
A program may use at most 128 MiB of HBM per device.

v0:
```python
import math

import jax
import jax.numpy as jnp
from jax import lax
from jax.sharding import PartitionSpec as P

WINDOW = 4


highest = lax.Precision.HIGHEST


def shifted(value, axis, by):
    size = lax.axis_size(axis)
    pairs = [(i, i + by) for i in range(size) if 0 <= i + by < size]
    return lax.ppermute(value, axis, pairs)


def bit_length(values, count_bits):
    length_sum = jnp.zeros(values.shape, jnp.int32)
    for bit_index in range(count_bits):
        length_sum = length_sum + (values >= 1 << bit_index).astype(jnp.int32)
    return length_sum


def shards(
    state_query,
    state_key,
    state_value,
    state_gate,
    log_decay,
    level_gate,
    norm_gain,
    attention_query,
    attention_key,
    attention_value,
):
    block_rows = state_query.shape[0]
    head_count = log_decay.shape[0]
    width_key = state_query.shape[1] // head_count
    width_value = state_value.shape[1] // head_count
    count_levels = level_gate.shape[1]
    shift_bits = block_rows.bit_length() - 1
    ctx_size = lax.axis_size("ctx")
    ctx_index = lax.axis_index("ctx")
    level_count = ctx_size.bit_length() - 1
    query_heads = state_query.reshape(block_rows, head_count, width_key)
    key_heads = state_key.reshape(block_rows, head_count, width_key)
    value_heads = state_value.reshape(block_rows, head_count, width_value)
    cum_decay = jnp.cumsum(log_decay, axis=1)
    local_positions = jnp.arange(block_rows, dtype=jnp.int32)
    causal = local_positions[:, None] >= local_positions[None, :]
    pair_level = bit_length(
        jnp.bitwise_xor(local_positions[:, None], local_positions[None, :]), count_levels
    )
    scores = jnp.einsum("ihd,jhd->hij", query_heads, key_heads, preferred_element_type=jnp.float32)
    decay_gap = jnp.where(causal[None], cum_decay[:, :, None] - cum_decay[:, None, :], -jnp.inf)
    level_scale = jnp.zeros(scores.shape, jnp.float32)
    for level_index in range(shift_bits + 1):
        level_scale = level_scale + jnp.where(
            (pair_level == level_index)[None], level_gate[:, level_index, :, None], 0.0
        )
    mixing = (scores * jnp.exp(decay_gap) * level_scale).astype(jnp.bfloat16)
    inside = jnp.einsum("hij,jhp->ihp", mixing, value_heads, preferred_element_type=jnp.float32)
    tail_decay = jnp.exp(cum_decay[:, -1:] - cum_decay)
    weighted_keys = (key_heads.astype(jnp.float32) * tail_decay.T[:, :, None]).astype(jnp.bfloat16)
    own_state = jnp.einsum(
        "jhd,jhp->hdp", weighted_keys, value_heads, preferred_element_type=jnp.float32
    )
    block_total = cum_decay[:, -1]
    all_totals = lax.all_gather(block_total[None, :], "ctx", axis=0, tiled=True)
    block_ends = jnp.cumsum(all_totals, axis=0)
    start_here = lax.dynamic_index_in_dim(block_ends, ctx_index, 0, keepdims=False) - block_total
    flat_state = own_state.reshape(1, head_count, width_key * width_value)
    level_numbers = jnp.arange(1, level_count + 1, dtype=jnp.int32)
    piece = lax.all_gather(flat_state, "ctx", axis=0, tiled=True)
    piece_rows = piece.shape[0]
    source = jnp.arange(piece_rows, dtype=jnp.int32)
    level_of = bit_length(jnp.bitwise_xor(source, ctx_index), count_levels)
    earlier = source < ctx_index
    decayed = jnp.exp(jnp.where(earlier[:, None], start_here[None, :] - block_ends, -jnp.inf))
    chosen = (level_of[None, :] == level_numbers[:, None]).astype(jnp.float32)
    weights = chosen[:, :, None] * decayed[None]
    level_states = jnp.einsum("mnh,nhx->mhx", weights, piece, precision=highest)
    level_states = level_states.reshape(level_count, head_count, width_key, width_value)
    level_low = level_states.astype(jnp.bfloat16)
    query_reach = (query_heads.astype(jnp.float32) * jnp.exp(cum_decay).T[:, :, None]).astype(
        jnp.bfloat16
    )
    across_levels = jnp.einsum(
        "ihd,mhdp->mihp", query_reach, level_low, preferred_element_type=jnp.float32
    )
    far_gate = level_gate[:, shift_bits + 1 : shift_bits + 1 + level_count, :]
    across = jnp.einsum("mihp,hmi->ihp", across_levels, far_gate)
    mixed_heads = (inside + across).reshape(block_rows, head_count * width_value)
    gated_heads = mixed_heads * jax.nn.silu(state_gate.astype(jnp.float32))
    square_sum = lax.psum(jnp.sum(gated_heads * gated_heads, axis=1), "head")
    total_width = head_count * width_value * lax.axis_size("head")
    norm_scale = lax.rsqrt(square_sum / total_width + 1e-05)
    mixer_output = (gated_heads * norm_scale[:, None] * norm_gain[None, :]).astype(jnp.bfloat16)
    own_pair = jnp.stack((attention_key, attention_value))
    earlier_pairs = []
    for step_index in range(1, WINDOW):
        earlier_pairs.append(shifted(own_pair, "ctx", step_index))
    window_pair = jnp.concatenate(earlier_pairs[::-1] + [own_pair], axis=1)
    window_positions = jnp.arange(WINDOW * block_rows, dtype=jnp.int32)
    key_block = window_positions // block_rows
    key_local = window_positions % block_rows
    distance = WINDOW - 1 - key_block
    allowed = (ctx_index - distance >= 0)[None, :] & (
        (distance > 0)[None, :] | (local_positions[:, None] >= key_local[None, :])
    )
    attention_heads = attention_query.reshape(block_rows, head_count, width_value)
    window_keys = window_pair[0].reshape(WINDOW * block_rows, head_count, width_value)
    window_values = window_pair[1].reshape(WINDOW * block_rows, head_count, width_value)
    logits = jnp.einsum(
        "ihd,jhd->hij", attention_heads, window_keys, preferred_element_type=jnp.float32
    ) * (1.0 / math.sqrt(width_value))
    logits = jnp.where(allowed[None], logits, -jnp.inf)
    row_max = jnp.max(logits, axis=2, keepdims=True)
    exponent = jnp.exp(logits - row_max)
    weights_low = (exponent / jnp.sum(exponent, axis=2, keepdims=True)).astype(jnp.bfloat16)
    attended = jnp.einsum(
        "hij,jhd->ihd", weights_low, window_values, preferred_element_type=jnp.float32
    )
    attention_output = attended.reshape(block_rows, head_count * width_value).astype(jnp.bfloat16)
    return (mixer_output, attention_output)


def solution(mesh):
    return jax.shard_map(
        shards,
        mesh=mesh,
        in_specs=(
            P("ctx", "head"),
            P("ctx", "head"),
            P("ctx", "head"),
            P("ctx", "head"),
            P("head", "ctx"),
            P("head", None, "ctx"),
            P("head"),
            P("ctx", "head"),
            P("ctx", "head"),
            P("ctx", "head"),
        ),
        out_specs=(P("ctx", "head"), P("ctx", "head")),
        check_vma=False,
    )
```

profile of v0, /device:TPU:16, one launch (start us, length us, event | category | flops | bytes accessed | tf_op | source)
XLA Modules:
  0.0 287.5 jit_solution(1422846004735788080)
XLA Ops:
  7.3 0.8 reshape.463
  8.1 1.2 reduce-window.6
  9.9 1.3 copy.89
  11.2 1.5 fusion.41
  12.8 0.8 reshape.466
  13.6 1.3 copy.69
  15.2 4.4 %collective-permute-start.2 = (bf16[2,512,512]{1,2,0:T(8,128)(2,1)S(1)}, bf16[2,512,512]{1,2,0:T(8,128)(2,1)}, u32[]{:S(2)}, u32[]{:S(2)}) collective-permute-start(bf16[2,512,512]{1,2,0:T(8,128)(2,1)S(1)} %pad_maximum_fusion), channel_id=1, source_target_pairs={{0,8},{8,16},{16,24},{24,32},{32,40},{40,48},{48,56},{56,64},{64,7... | collective-permute-start | bytes 3145736 | tf_op jit(solution)/shard_map/ppermute | solution.py:17
  19.6 4.7 %collective-permute-start.1 = (bf16[2,512,512]{1,2,0:T(8,128)(2,1)S(1)}, bf16[2,512,512]{1,2,0:T(8,128)(2,1)}, u32[]{:S(2)}, u32[]{:S(2)}) collective-permute-start(bf16[2,512,512]{1,2,0:T(8,128)(2,1)S(1)} %pad_maximum_fusion), channel_id=1, source_target_pairs={{0,16},{8,24},{16,32},{24,40},{32,48},{40,56},{48,64},{56,72},{64,... | collective-permute-start | bytes 3145736 | tf_op jit(solution)/shard_map/ppermute | solution.py:17
  24.3 4.7 %collective-permute-start = (bf16[2,512,512]{1,2,0:T(8,128)(2,1)S(1)}, bf16[2,512,512]{1,2,0:T(8,128)(2,1)}, u32[]{:S(2)}, u32[]{:S(2)}) collective-permute-start(bf16[2,512,512]{1,2,0:T(8,128)(2,1)S(1)} %pad_maximum_fusion), channel_id=1, source_target_pairs={{0,24},{8,32},{16,40},{24,48},{32,56},{40,64},{48,72},{56,80},{64,... | collective-permute-start | bytes 3145736 | tf_op jit(solution)/shard_map/ppermute | solution.py:17
  28.9 0.6 dynamic-slice
  30.3 179.4 %all-reduce = f32[128]{0:T(128)S(1)} all-reduce(f32[128]{0:T(128)S(1)} %bitcast_dynamic-update-slice_fusion), channel_id=2, replica_groups=mesh['ctx'=32,'head'=8] {'ctx'}, use_global_device_ids=true, to_apply=%add | all-reduce | flops 128 | bytes 1024
  210.1 0.3 broadcast_compare_fusion.9
  210.4 1.2 broadcast_compare_fusion.7
  211.5 1.1 broadcast_compare_fusion.5
  212.7 1.1 broadcast_compare_fusion.3
  213.8 1.2 broadcast_compare_fusion.1
  215.0 0.6 slice_bitcast_fusion.10
  215.6 1.1 iota_compare_fusion.1
  216.7 2.8 fusion.10
  219.6 2.1 maximum_maximum_fusion
  221.7 1.8 fusion.105
  223.5 12.3 %fusion.106 = (f32[4,512]{1,0:T(4,128)}, f32[4,512,2048]{1,2,0:T(8,128)}) fusion(pred[512,2048]{0,1:T(8,128)(4,1)} %fusion.10, bf16[2048,4,128]{0,2,1:T(8,128)(2,1)} %bitcast.143, bf16[512,512]{1,0:T(8,128)(2,1)S(1)} %copy-done), kind=kOutput, calls=%fused_computation.171 | convolution fusion | flops 1090521088 | bytes 20455424 | tf_op jit(solution)/shard_map/sub | solution.py:122
  235.8 7.0 %fusion.16 = bf16[4,128,512]{2,1,0:T(8,128)(2,1)S(1)} fusion(bf16[2048,4,128]{0,2,1:T(8,128)(2,1)S(1)} %bitcast.142, f32[4,512,2048]{1,2,0:T(8,128)} %get-tuple-element.25, f32[4,512]{1,0:T(4,128)} %get-tuple-element.24), kind=kOutput, calls=%fused_computation.25 | convolution fusion | flops 1082392576 | bytes 19406848 | tf_op jit(solution)/shard_map/hij,jhd->ihd/dot_general | solution.py:124
  242.9 1.0 copy.74
  243.9 12.3 %fusion.1 = bf16[5,4,16384]{2,0,1:T(8,128)(2,1)S(1)} fusion(f32[32,4,16384]{2,1,0:T(4,128)} %all-gather.3.cloned.1.call-done, f32[32,4]{0,1:T(4,128)S(1)} %select_exponential_fusion, f32[5,32]{1,0:T(8,128)S(1)} %compare_convert_fusion), kind=kOutput, calls=%fused_computation.2 | convolution fusion | flops 126157440 | bytes 9045120 | tf_op jit(solution)/shard_map/mnh,nhx->mhx/dot_general | solution.py:85
  256.1 1.0 reshape.479
  257.2 2.1 fusion.8
  259.2 9.4 %fusion.15 = f32[512,4,128]{0,2,1:T(8,128)S(1)} fusion(f32[512,4,128]{0,2,1:T(8,128)} %fusion.8, bf16[512,4,128]{0,2,1:T(8,128)(2,1)} %bitcast.146, f32[4,512]{1,0:T(4,128)} %get-tuple-element.21, f32[4,512]{1,0:T(4,128)S(1)} %get-tuple-element.13, f32[4,512]{1,0:T(4,128)S(1)} %get-tuple-element.14, f32[4,512]{1,0:T(4,128)S(1)} %get-tuple-element.15, ...), kind=kOutput, calls=%fused_computation.22 | convolution fusion | flops 562298880 | bytes 6643712 | tf_op jit(solution)/shard_map/hij,jhp->ihp/dot_general | solution.py:65
  268.7 0.3 copy.68
  269.0 0.4 multiply_reduce_fusion
  269.4 10.1 %psum.7 = f32[512]{0:T(512)S(1)} all-reduce(f32[512]{0:T(512)S(1)} %multiply_reduce_fusion), channel_id=1, replica_groups=mesh['ctx'=32,'head'=8] {'head'}, use_global_device_ids=true, to_apply=%region_4.5 | all-reduce | flops 512 | bytes 4096 | tf_op jit(solution)/shard_map/psum | solution.py:98
  279.5 1.2 multiply_convert_fusion.1
  (47 shorter events, 1.7 us)
Async XLA Ops:
  7.2 216.3 %copy-start = (bf16[512,512]{1,0:T(8,128)(2,1)S(1)}, bf16[512,512]{1,0:T(8,128)(2,1)}, u32[]{:S(2)}) copy-start(bf16[512,512]{1,0:T(8,128)(2,1)} %param.17) | copy-start | bytes 1572868
  7.2 21.8 %copy-start.7 = (u32[256]{0:T(256)S(1)}, u32[256]{0:T(256)}, u32[]{:S(2)}) copy-start(u32[256]{0:T(256)} %constant.138) | copy-start | bytes 3076
  7.2 7.7 %copy-start.2 = (bf16[512,512]{1,0:T(8,128)(2,1)S(1)}, bf16[512,512]{1,0:T(8,128)(2,1)}, u32[]{:S(2)}) copy-start(bf16[512,512]{1,0:T(8,128)(2,1)} %param.19) | copy-start | bytes 1572868
  7.2 202.9 %copy-start.4 = (f32[4,20,512]{2,0,1:T(4,128)S(1)}, f32[4,20,512]{2,0,1:T(4,128)}, u32[]{:S(2)}) copy-start(f32[4,20,512]{2,0,1:T(4,128)} %param.15) | copy-start | bytes 491524
  7.2 236.6 %all-gather.3.cloned.1.call-start = ((), (), s32[]{:S(2)}) async-start(), calls=%async_computation | async-start | bytes 8650752 | tf_op jit(solution)/shard_map/all_gather | solution.py:77
  11.2 2.4 copy-start.3
  15.2 204.4 %collective-permute-start.2 = (bf16[2,512,512]{1,2,0:T(8,128)(2,1)S(1)}, bf16[2,512,512]{1,2,0:T(8,128)(2,1)}, u32[]{:S(2)}, u32[]{:S(2)}) collective-permute-start(bf16[2,512,512]{1,2,0:T(8,128)(2,1)S(1)} %pad_maximum_fusion), channel_id=1, source_target_pairs={{0,8},{8,16},{16,24},{24,32},{32,40},{40,48},{48,56},{56,64},{64,7... | collective-permute-start | bytes 3145736 | tf_op jit(solution)/shard_map/ppermute | solution.py:17
  19.6 200.0 %collective-permute-start.1 = (bf16[2,512,512]{1,2,0:T(8,128)(2,1)S(1)}, bf16[2,512,512]{1,2,0:T(8,128)(2,1)}, u32[]{:S(2)}, u32[]{:S(2)}) collective-permute-start(bf16[2,512,512]{1,2,0:T(8,128)(2,1)S(1)} %pad_maximum_fusion), channel_id=1, source_target_pairs={{0,16},{8,24},{16,32},{24,40},{32,48},{40,56},{48,64},{56,72},{64,... | collective-permute-start | bytes 3145736 | tf_op jit(solution)/shard_map/ppermute | solution.py:17
  24.3 195.3 %collective-permute-start = (bf16[2,512,512]{1,2,0:T(8,128)(2,1)S(1)}, bf16[2,512,512]{1,2,0:T(8,128)(2,1)}, u32[]{:S(2)}, u32[]{:S(2)}) collective-permute-start(bf16[2,512,512]{1,2,0:T(8,128)(2,1)S(1)} %pad_maximum_fusion), channel_id=1, source_target_pairs={{0,24},{8,32},{16,40},{24,48},{32,56},{40,64},{48,72},{56,80},{64,... | collective-permute-start | bytes 3145736 | tf_op jit(solution)/shard_map/ppermute | solution.py:17
  243.9 13.3 %copy-start.6 = (bf16[512,512]{1,0:T(8,128)(2,1)S(1)}, bf16[512,512]{1,0:T(8,128)(2,1)}, u32[]{:S(2)}) copy-start(bf16[512,512]{1,0:T(8,128)(2,1)} %param.10) | copy-start | bytes 1572868
  259.2 9.8 %copy-start.1 = (bf16[512,512]{1,0:T(8,128)(2,1)S(1)}, bf16[512,512]{1,0:T(8,128)(2,1)}, u32[]{:S(2)}) copy-start(bf16[512,512]{1,0:T(8,128)(2,1)} %param.13) | copy-start | bytes 1572868
  259.2 20.3 %copy-start.5 = (f32[512]{0:T(512)S(1)}, f32[512]{0:T(512)}, u32[]{:S(2)}) copy-start(f32[512]{0:T(512)} %param.16) | copy-start | bytes 6148
Sparse Core Ops, SparseCore 0:
  13.7 142.0 all-gather.2
where the time goes:
time: 291 us; the launch traced here: 288 us
  blocking collectives  189 us (65%)
  matrix products  44.6 us (15%)
  between operations  14.9 us (5%)
  other arithmetic  14.4 us (5%)
  starting transfers between devices  13.8 us (5%)
  local copies, waits for them, and re-layouts  10.4 us (4%)
    unnamed x1, blocking collectives  179 us
    ppermute x3, starting transfers between devices, shifted(): return lax.ppermute(value, axis, pairs)  13.7 us
    sub x1, matrix products, shards(): exponent = jnp.exp(logits - row_max)  12.3 us
    dot_general x1, matrix products, shards(): level_states = jnp.einsum('mnh,nhx->mhx', weights, piece, precision=highest)  12.3 us
    psum x1, blocking collectives, shards(): square_sum = lax.psum(jnp.sum(gated_heads * gated_heads, axis=1), 'head')  10.1 us
    dot_general x1, matrix products, shards(): jnp.einsum('hij,jhp->ihp', mixing, value_heads, preferred_element_type=jn...  9.43 us
    dot_general x1, matrix products, shards(): jnp.einsum('hij,jhd->ihd', weights_low, window_values, preferred_element_...  7.04 us
  transfers between devices with their start and end apart: 4, of which 0 were waited for; matrix products, arithmetic and copies ran while one was open for 13% of the time, Pallas kernels for 0%

commit v1 on v0

v1 whole, which is shorter than its diff:
```python
import functools
import math

import jax
import jax.numpy as jnp
from jax import lax
from jax.experimental import pallas as pl
from jax.experimental.pallas import tpu as pltpu
from jax.sharding import PartitionSpec as P

MESH = pl.DeviceIdType.MESH
ROW = 4
F32 = jnp.float32
BF16 = jnp.bfloat16
NEG = -1e30


def nt_dot(a, b):
    return lax.dot_general(a, b, (((1,), (1,)), ((), ())), preferred_element_type=F32)


def tn_dot(a, b):
    return lax.dot_general(a, b, (((0,), (0,)), ((), ())), preferred_element_type=F32)


def kernel(
    zn,
    hn,
    sq_hbm,
    sk_hbm,
    sv_hbm,
    sg_hbm,
    ld_ref,
    lg_ref,
    gain_ref,
    aq_hbm,
    ak_hbm,
    av_hbm,
    mo_hbm,
    ao_hbm,
    sq,
    sk,
    sv,
    sg,
    qbuf,
    kbuf,
    vbuf,
    obuf,
    grow,
    gcol,
    mixed,
    gated,
    mout,
    ssend,
    srecv,
    tsend,
    trecv,
    rsend,
    rrecv,
    trsend,
    trrecv,
    lsend,
    lrecv,
    nsend,
    nrecv,
    loc_sem,
    x_send,
    x_recv,
    h_send,
    h_recv,
    s_send,
    s_recv,
    r_send,
    r_recv,
    l_send,
    l_recv,
    n_send,
    n_recv,
    o_send,
    o_recv,
    out_sem,
):
    me = lax.axis_index("ctx")
    mh = lax.axis_index("head")
    z = me // ROW
    x = me % ROW
    tok = qbuf.shape[1]
    hd = qbuf.shape[2]
    chunk = 128
    chunks = tok // chunk

    def rowdev(d):
        return z * ROW + (x + d) % ROW

    def cols(h):
        return pl.ds(pl.multiple_of(h * hd, hd), hd)

    state_in = [
        pltpu.make_async_copy(src, dst, loc_sem.at[i])
        for i, (src, dst) in enumerate(((sk_hbm, sk), (sv_hbm, sv), (sq_hbm, sq), (sg_hbm, sg)))
    ]
    for c in state_in:
        c.start()
    att = ((ak_hbm, kbuf, 3), (av_hbm, vbuf, 3), (aq_hbm, qbuf, 0))
    own_in = [
        pltpu.make_async_copy(src.at[:, cols(x)], dst.at[base + x], loc_sem.at[4 + i])
        for i, (src, dst, base) in enumerate(att)
    ]
    for c in own_in:
        c.start()

    rrecv[...] = jnp.zeros_like(rrecv)
    trrecv[...] = jnp.zeros_like(trrecv)

    @pl.when(x != 3)
    def _():
        lrecv[:, 4] = jnp.zeros_like(lrecv[:, 4])

    @pl.when(z == 0)
    def _():
        kbuf[0:3] = jnp.zeros((3, tok, hd), BF16)
        vbuf[0:3] = jnp.zeros((3, tok, hd), BF16)

    barrier = pltpu.get_barrier_semaphore()
    for d in range(1, ROW):
        pl.semaphore_signal(barrier, inc=1, device_id={"ctx": rowdev(d)}, device_id_type=MESH)
    for d in range(1, zn):
        pl.semaphore_signal(
            barrier, inc=1, device_id={"ctx": ((z + d) % zn) * ROW + x}, device_id_type=MESH
        )
    for d in range(1, hn):
        pl.semaphore_signal(barrier, inc=1, device_id={"head": (mh + d) % hn}, device_id_type=MESH)
    pl.semaphore_wait(barrier, ROW - 1 + zn - 1 + hn - 1)

    def x_copy(t, d):
        src, dst, base = att[t]
        return pltpu.make_async_remote_copy(
            src_ref=src.at[:, cols((x + d) % ROW)],
            dst_ref=dst.at[base + x],
            send_sem=x_send.at[t, d - 1],
            recv_sem=x_recv.at[t, d - 1],
            device_id={"ctx": rowdev(d)},
            device_id_type=MESH,
        )

    def x_wait(t, d):
        src, dst, base = att[t]
        pltpu.make_async_remote_copy(
            src_ref=src.at[:, cols((x + d) % ROW)],
            dst_ref=dst.at[base + (x + ROW - d) % ROW],
            send_sem=x_send.at[t, d - 1],
            recv_sem=x_recv.at[t, d - 1],
            device_id={"ctx": rowdev(d)},
            device_id_type=MESH,
        ).wait_recv()

    def halo_own(t):
        src, dst, _ = att[t]
        return pltpu.make_async_remote_copy(
            src_ref=src.at[:, cols(x)],
            dst_ref=dst.at[(x + ROW - 1) % ROW],
            send_sem=h_send.at[t, 0],
            recv_sem=h_recv.at[t, (x + ROW - 1) % ROW],
            device_id={"ctx": me + ROW},
            device_id_type=MESH,
        )

    def halo_relay(t, d):
        dst = att[t][1]
        block = (x + ROW - d) % ROW
        return pltpu.make_async_remote_copy(
            src_ref=dst.at[3 + block],
            dst_ref=dst.at[(block + ROW - 1) % ROW],
            send_sem=h_send.at[t, d],
            recv_sem=h_recv.at[t, (block + ROW - 1) % ROW],
            device_id={"ctx": me + ROW},
            device_id_type=MESH,
        )

    def relay_if(d):
        return ((x + ROW - d) % ROW >= 1) & (z < zn - 1)

    def halo_wait(t, slot):
        dst = att[t][1]
        pltpu.make_async_remote_copy(
            src_ref=dst.at[slot],
            dst_ref=dst.at[slot],
            send_sem=h_send.at[t, 0],
            recv_sem=h_recv.at[t, slot],
            device_id={"ctx": (me + ROW) % (zn * ROW)},
            device_id_type=MESH,
        ).wait_recv()

    def s_copies(d):
        p = (x + d) % ROW
        return [
            pltpu.make_async_remote_copy(
                src_ref=src.at[p],
                dst_ref=dst.at[x],
                send_sem=s_send.at[i, d - 1],
                recv_sem=s_recv.at[i, d - 1],
                device_id={"ctx": rowdev(d)},
                device_id_type=MESH,
            )
            for i, (src, dst) in enumerate(((ssend, srecv), (tsend, trecv)))
        ]

    def r_copies(d):
        return [
            pltpu.make_async_remote_copy(
                src_ref=src,
                dst_ref=dst.at[d - 1],
                send_sem=r_send.at[i, d - 1],
                recv_sem=r_recv.at[i, d - 1],
                device_id={"ctx": ((z + d) % zn) * ROW + x},
                device_id_type=MESH,
            )
            for i, (src, dst) in enumerate(((rsend, rrecv), (trsend, trrecv)))
        ]

    def l_copy(i, d):
        part = pl.ds(0, 4) if i == 0 else pl.ds(4, 1)
        return pltpu.make_async_remote_copy(
            src_ref=lsend.at[d, part],
            dst_ref=lrecv.at[x, part],
            send_sem=l_send.at[i, d - 1],
            recv_sem=l_recv.at[i, d - 1],
            device_id={"ctx": rowdev(d)},
            device_id_type=MESH,
        )

    def n_copy(d):
        return pltpu.make_async_remote_copy(
            src_ref=nsend,
            dst_ref=nrecv.at[d - 1],
            send_sem=n_send.at[d - 1],
            recv_sem=n_recv.at[d - 1],
            device_id={"head": (mh + d) % hn},
            device_id_type=MESH,
        )

    def o_copy(j):
        return pltpu.make_async_remote_copy(
            src_ref=obuf.at[j],
            dst_ref=ao_hbm.at[:, cols(x)],
            send_sem=o_send.at[j],
            recv_sem=o_recv.at[x],
            device_id={"ctx": z * ROW + j},
            device_id_type=MESH,
        )

    def o_local(j):
        return pltpu.make_async_copy(obuf.at[j], ao_hbm.at[:, cols(x)], out_sem.at[1])

    for d in (1, 3, 2):
        x_copy(0, d).start()
    own_halo = (x >= 1) & (z < zn - 1)

    @pl.when(own_halo)
    def _():
        halo_own(0).start()
        halo_own(1).start()

    lane = lax.broadcasted_iota(jnp.int32, (8, tok), 1)
    cum = jnp.concatenate([ld_ref[...], jnp.zeros((8 - ROW, tok), F32)], axis=0)
    shift = 1
    while shift < tok:
        cum = cum + jnp.where(lane >= shift, pltpu.roll(cum, shift, axis=1), 0.0)
        shift *= 2
    last = cum[:, tok - 1 : tok]
    tail = jnp.exp(last - cum)
    reach = jnp.exp(cum)
    for h in range(ROW):
        grow[h, 0:20, :] = lg_ref[h]
        grow[h, 20:21, :] = cum[h : h + 1]
        grow[h, 21:22, :] = tail[h : h + 1]
        grow[h, 22:23, :] = reach[h : h + 1]
        grow[h, 23:24, :] = cum[h : h + 1]
        grow[h, 24:32, :] = cum
        tsend[h] = jnp.broadcast_to(last[h : h + 1], (8, 128))
        gcol[h] = grow[h].T

    state_in[0].wait()
    state_in[1].wait()

    def summary(h, _):
        kf = sk[:, cols(h)].astype(F32)
        low = (kf * gcol[h, :, 21:22]).astype(BF16)
        ssend[h] = tn_dot(low, sv[:, cols(h)]).astype(BF16)
        return 0

    lax.fori_loop(0, ROW, summary, 0)
    for d in (1, 3, 2):
        for c in s_copies(d):
            c.start()
    for t in (1, 2):
        for d in (1, 3, 2):
            x_copy(t, d).start()
    srecv[x] = ssend[x]
    trecv[x] = tsend[x]

    state_in[2].wait()
    state_in[3].wait()
    row_i = lax.broadcasted_iota(jnp.int32, (chunk, chunk), 0)
    col_i = lax.broadcasted_iota(jnp.int32, (chunk, chunk), 1)

    apart = row_i ^ col_i

    def inside(h, _):
        hc = cols(h)
        crow = grow[h, 20:21, :]
        for i in range(chunks):
            rows = pl.ds(i * chunk, chunk)
            g = gcol[h, rows, :]
            ccol = g[:, 20:21]
            scores = nt_dot(sq[rows, hc], sk[0 : (i + 1) * chunk, hc])
            parts = []
            for j in range(i + 1):
                s = scores[:, j * chunk : (j + 1) * chunk]
                gap = ccol - crow[:, j * chunk : (j + 1) * chunk]
                if j < i:
                    level = (i ^ j).bit_length() + 7
                    m = s * jnp.exp(gap) * g[:, level : level + 1]
                else:
                    gate = jnp.broadcast_to(g[:, 0:1], (chunk, chunk))
                    for level in range(1, 8):
                        gate = jnp.where(apart >= 1 << (level - 1), g[:, level : level + 1], gate)
                    seen = row_i >= col_i
                    m = jnp.where(seen, s * jnp.exp(jnp.where(seen, gap, 0.0)) * gate, 0.0)
                parts.append(m.astype(BF16))
            low = parts[0] if i == 0 else jnp.concatenate(parts, axis=1)
            mixed[h, rows, :] = jnp.dot(
                low, sv[0 : (i + 1) * chunk, hc], preferred_element_type=F32
            )
        return 0

    lax.fori_loop(0, ROW, inside, 0)

    for d in range(1, ROW):
        p = (x + ROW - d) % ROW
        for i, (src, dst) in enumerate(((ssend, srecv), (tsend, trecv))):
            pltpu.make_async_remote_copy(
                src_ref=src.at[p],
                dst_ref=dst.at[p],
                send_sem=s_send.at[i, d - 1],
                recv_sem=s_recv.at[i, d - 1],
                device_id={"ctx": rowdev(d)},
                device_id_type=MESH,
            ).wait_recv()
    tot = [trecv[i] for i in range(ROW)]
    st = [srecv[i].astype(F32) for i in range(ROW)]
    pair = st[0] * jnp.exp(tot[1][0:1]) + st[1]
    row_state = (
        pair * jnp.exp((tot[2] + tot[3])[0:1]) + st[2] * jnp.exp(tot[3][0:1]) + st[3]
    )
    rsend[...] = row_state.astype(BF16)
    trsend[...] = tot[0] + tot[1] + tot[2] + tot[3]
    for d in range(1, zn):

        @pl.when(z + d < zn)
        def _():
            for c in r_copies(d):
                c.start()

    for c in own_in:
        c.wait()
    for d in (1, 3, 2):
        for t in (0, 1):
            x_wait(t, d)

            @pl.when(relay_if(d))
            def _():
                halo_relay(t, d).start()

    for d in (1, 3, 2):
        x_wait(2, d)

    kappa = math.log2(math.e) / math.sqrt(hd)
    qrows = 256
    absent = jnp.where(z == 0, NEG, 0.0).astype(F32)

    def attend(j):
        def body(i, _):
            first = pl.multiple_of(i * qrows, qrows)
            q = qbuf[j, pl.ds(first, qrows), :]
            logits = []
            for s in range(ROW):
                part = nt_dot(q, kbuf[j + s])
                if j + s < 3:
                    part = part + absent
                if s == ROW - 1:
                    r = lax.broadcasted_iota(jnp.int32, (qrows, tok), 0) + first
                    c = lax.broadcasted_iota(jnp.int32, (qrows, tok), 1)
                    part = jnp.where(r >= c, part, NEG)
                logits.append(part)
            top = jnp.maximum(
                jnp.maximum(logits[0], logits[1]), jnp.maximum(logits[2], logits[3])
            )
            top = jnp.max(top, axis=1, keepdims=True)
            weights = [jnp.exp2((part - top) * kappa) for part in logits]
            total = jnp.sum(
                (weights[0] + weights[1]) + (weights[2] + weights[3]), axis=1, keepdims=True
            )
            out = None
            for s in range(ROW):
                term = jnp.dot(
                    weights[s].astype(BF16), vbuf[j + s], preferred_element_type=F32
                )
                out = term if out is None else out + term
            obuf[j, pl.ds(first, qrows), :] = (out / total).astype(BF16)
            return 0

        lax.fori_loop(0, tok // qrows, body, 0)

        @pl.when(x != j)
        def _():
            o_copy(j).start()

        @pl.when(x == j)
        def _():
            o_local(j).start()

    attend(3)

    for d in range(1, zn):

        @pl.when(z - d >= 0)
        def _():
            for c in r_copies(d):
                c.wait_recv()

    levels = [jnp.zeros((hd, hd), F32) for _ in range(3)]
    decay = jnp.zeros((8, 128), F32)
    for d in range(1, zn):
        other = z + zn - d
        near2 = (z + zn) // 2 == other // 2
        near4 = (z + zn) // 4 == other // 4
        w = jnp.exp(decay)[0:1]
        held = rrecv[d - 1].astype(F32)
        levels[0] = levels[0] + jnp.where(near2, w, 0.0) * held
        levels[1] = levels[1] + jnp.where(near4 & ~near2, w, 0.0) * held
        levels[2] = levels[2] + jnp.where(near4, 0.0, w) * held
        decay = decay + trrecv[d - 1]
    for d in (0, 1, 3, 2):
        xp = (x + d) % ROW
        before = (
            jnp.where(xp >= 1, tot[0], 0.0)
            + jnp.where(xp >= 2, tot[1], 0.0)
            + jnp.where(xp >= 3, tot[2], 0.0)
        )
        w = jnp.exp(before)[0:1]
        for m in range(3):
            lsend[d, m] = (levels[m] * w).astype(BF16)
        near = jnp.where(xp == 1, st[0], jnp.where(xp == 2, pair, jnp.where(xp == 3, st[2], 0.0)))
        lsend[d, 3] = near.astype(BF16)
        lsend[d, 4] = (pair * jnp.exp(tot[2][0:1])).astype(BF16)
        if d > 0:
            l_copy(0, d).start()

            @pl.when(xp == 3)
            def _():
                l_copy(1, d).start()

    lrecv[x, 0:4] = lsend[0, 0:4]

    @pl.when(x == 3)
    def _():
        lrecv[x, 4] = lsend[0, 4]

    def halos(slot):
        @pl.when(z > 0)
        def _():
            for t in (0, 1):
                halo_wait(t, slot)

    halos(2)
    attend(2)

    for d in range(1, ROW):
        p = (x + ROW - d) % ROW
        pltpu.make_async_remote_copy(
            src_ref=lsend.at[d, pl.ds(0, 4)],
            dst_ref=lrecv.at[p, pl.ds(0, 4)],
            send_sem=l_send.at[0, d - 1],
            recv_sem=l_recv.at[0, d - 1],
            device_id={"ctx": rowdev(d)},
            device_id_type=MESH,
        ).wait_recv()

        @pl.when(x == 3)
        def _():
            pltpu.make_async_remote_copy(
                src_ref=lsend.at[d, pl.ds(4, 1)],
                dst_ref=lrecv.at[p, pl.ds(4, 1)],
                send_sem=l_send.at[1, d - 1],
                recv_sem=l_recv.at[1, d - 1],
                device_id={"ctx": rowdev(d)},
                device_id_type=MESH,
            ).wait_recv()

    def across(h, acc):
        hc = cols(h)
        squares = []
        for i in range(chunks):
            rows = pl.ds(i * chunk, chunk)
            g = gcol[h, rows, :]
            qf = sq[rows, hc].astype(F32) * g[:, 22:23]
            near = jnp.where(x == 2, g[:, 11:12], g[:, 10:11])
            low = jnp.concatenate(
                [
                    (qf * gate).astype(BF16)
                    for gate in (g[:, 12:13], g[:, 13:14], g[:, 14:15], near, g[:, 11:12])
                ],
                axis=1,
            )
            far = jnp.dot(low, lrecv[h].reshape(5 * hd, hd), preferred_element_type=F32)
            v = sg[rows, hc].astype(F32)
            out = (mixed[h, rows, :] + far) * (v / (1.0 + jnp.exp(-v)))
            gated[rows, hc] = out
            squares.append(out * out)
        return tuple(a + s for a, s in zip(acc, squares))

    acc = lax.fori_loop(
        0, ROW, across, tuple(jnp.zeros((chunk, hd), F32) for _ in range(chunks))
    )
    nsend[...] = jnp.zeros_like(nsend)
    for i in range(chunks):
        nsend[i : i + 1, :] = jnp.sum(acc[i].T, axis=0, keepdims=True)
    for d in range(1, hn):
        n_copy(d).start()

    halos(1)
    attend(1)
    halos(0)
    attend(0)

    total = nsend[...]
    for d in range(1, hn):
        n_copy(d).wait_recv()
        total = total + nrecv[d - 1]
    scale = lax.rsqrt(total / (hn * ROW * hd) + 1e-05)
    for i in range(chunks):
        rows = pl.ds(i * chunk, chunk)
        scale_col = jnp.broadcast_to(scale[i : i + 1], (chunk, chunk)).T
        for h in range(ROW):
            hs = slice(h * hd, (h + 1) * hd)
            mout[rows, hs] = (gated[rows, hs] * scale_col * gain_ref[:, hs]).astype(BF16)
    mix_out = pltpu.make_async_copy(mout, mo_hbm, out_sem.at[0])
    mix_out.start()

    for d in range(1, ROW):
        for t in range(3):
            x_copy(t, d).wait_send()
        for c in s_copies(d):
            c.wait_send()
        l_copy(0, d).wait_send()

        @pl.when((x + d) % ROW == 3)
        def _():
            l_copy(1, d).wait_send()

        @pl.when(relay_if(d))
        def _():
            for t in (0, 1):
                halo_relay(t, d).wait_send()

    @pl.when(own_halo)
    def _():
        for t in (0, 1):
            halo_own(t).wait_send()

    for d in range(1, zn):

        @pl.when(z + d < zn)
        def _():
            for c in r_copies(d):
                c.wait_send()

    for d in range(1, hn):
        n_copy(d).wait_send()
    for j in range(ROW):

        @pl.when(x != j)
        def _():
            o_copy(j).wait_send()
            pltpu.make_async_remote_copy(
                src_ref=obuf.at[j],
                dst_ref=ao_hbm.at[:, cols(j)],
                send_sem=o_send.at[j],
                recv_sem=o_recv.at[j],
                device_id={"ctx": z * ROW + j},
                device_id_type=MESH,
            ).wait_recv()

        @pl.when(x == j)
        def _():
            o_local(j).wait()

    mix_out.wait()


def shards(zn, hn, sq, sk, sv, sg, ld, lg, gain, aq, ak, av):
    tok = sq.shape[0]
    heads = ld.shape[0]
    hd = sq.shape[1] // heads
    wide = heads * hd
    dma = pltpu.SemaphoreType.DMA
    vm = pltpu.VMEM
    anywhere = pl.BlockSpec(memory_space=pl.ANY)
    here = pl.BlockSpec(memory_space=pltpu.VMEM)
    out = jax.ShapeDtypeStruct((tok, wide), BF16)
    return pl.pallas_call(
        functools.partial(kernel, zn, hn),
        out_shape=(out, out),
        in_specs=[anywhere] * 4 + [here] * 3 + [anywhere] * 3,
        out_specs=(anywhere, anywhere),
        scratch_shapes=[
            vm((tok, wide), BF16),
            vm((tok, wide), BF16),
            vm((tok, wide), BF16),
            vm((tok, wide), BF16),
            vm((4, tok, hd), BF16),
            vm((7, tok, hd), BF16),
            vm((7, tok, hd), BF16),
            vm((4, tok, hd), BF16),
            vm((heads, 32, tok), F32),
            vm((heads, tok, 32), F32),
            vm((heads, tok, hd), F32),
            vm((tok, wide), F32),
            vm((tok, wide), BF16),
            vm((4, hd, hd), BF16),
            vm((4, hd, hd), BF16),
            vm((4, 8, 128), F32),
            vm((4, 8, 128), F32),
            vm((hd, hd), BF16),
            vm((max(zn - 1, 1), hd, hd), BF16),
            vm((8, 128), F32),
            vm((max(zn - 1, 1), 8, 128), F32),
            vm((4, 5, hd, hd), BF16),
            vm((4, 5, hd, hd), BF16),
            vm((8, 128), F32),
            vm((max(hn - 1, 1), 8, 128), F32),
            dma((7,)),
            dma((3, 3)),
            dma((3, 3)),
            dma((2, 4)),
            dma((2, 4)),
            dma((2, 3)),
            dma((2, 3)),
            dma((2, max(zn - 1, 1))),
            dma((2, max(zn - 1, 1))),
            dma((2, 3)),
            dma((2, 3)),
            dma((max(hn - 1, 1),)),
            dma((max(hn - 1, 1),)),
            dma((4,)),
            dma((4,)),
            dma((2,)),
        ],
        compiler_params=pltpu.CompilerParams(
            collective_id=0, has_side_effects=True, vmem_limit_bytes=48 * 1024 * 1024
        ),
        cost_estimate=pl.CostEstimate(
            flops=3_000_000_000, bytes_accessed=5_000_000, transcendentals=5_000_000
        ),
    )(sq, sk, sv, sg, ld, lg, gain.reshape(1, wide), aq, ak, av)


def solution(mesh):
    zn = mesh.shape["ctx"] // ROW
    hn = mesh.shape["head"]
    return jax.shard_map(
        functools.partial(shards, zn, hn),
        mesh=mesh,
        in_specs=(
            P("ctx", "head"),
            P("ctx", "head"),
            P("ctx", "head"),
            P("ctx", "head"),
            P("head", "ctx"),
            P("head", None, "ctx"),
            P("head"),
            P("ctx", "head"),
            P("ctx", "head"),
            P("ctx", "head"),
        ),
        out_specs=(P("ctx", "head"), P("ctx", "head")),
        check_vma=False,
    )
```

time: 291 us -> 70.8 us (0.24)
  blocking collectives: 189 us -> 0 us
  Pallas kernels: 0 us -> 59.6 us
  matrix products: 44.6 us -> 0 us
  other arithmetic: 14.4 us -> 0 us
  between operations: 14.9 us -> 0.69 us
  starting transfers between devices: 13.8 us -> 0 us
    unnamed x1 -> x0, blocking collectives: 179 us -> none
    pallas_call x0 -> x1, Pallas kernels: none -> 59.6 us  [shards(): pl.pallas_call(functools.partial(kernel, zn, hn), out_shape=(out, out), i...]
    dot_general x5 -> x0, matrix products: 32.3 us -> none  [the longest x1 12.3 us: shards(): level_states = jnp.einsum('mnh,nhx->mhx', weights, piece, precision=highest)]
    ppermute x3 -> x0, starting transfers between devices: 13.7 us -> none  [shifted(): return lax.ppermute(value, axis, pairs)]
    sub x1 -> x0, matrix products: 12.3 us -> none  [shards(): exponent = jnp.exp(logits - row_max)]
    psum x1 -> x0, blocking collectives: 10.1 us -> none  [shards(): square_sum = lax.psum(jnp.sum(gated_heads * gated_heads, axis=1), 'head')]
    unnamed x26 -> x21, local copies, waits for them, and re-layouts: 3.33 us -> 9.86 us
    eq x5 -> x0, other arithmetic: 4.86 us -> none  [shards(): pair_level == level_index]
  transfers between devices with their start and end apart: 4 -> 0, of which waited for: 0 -> 0; matrix products, arithmetic and copies ran while one was open for 13% -> 0% of each run, Pallas kernels for 0% -> 0%
where the time goes in v1:
time: 70.8 us; the launch traced here: 70.1 us
  Pallas kernels  59.6 us (84%)
  local copies, waits for them, and re-layouts  9.86 us (14%)
    pallas_call x1, Pallas kernels, shards(): pl.pallas_call(functools.partial(kernel, zn, hn), out_shape=(out, out), i...  59.6 us
    unnamed x21, local copies, waits for them, and re-layouts  9.86 us

profile of v1, /device:TPU:16, one launch (start us, length us, event | category | flops | bytes accessed | tf_op | source)
XLA Modules:
  0.0 70.1 jit_solution(8793380741644149291)
XLA Ops:
  0.6 0.0 copy-start.7
  0.6 0.0 copy-start.8
  0.7 1.0 %copy.12.lg_ref = f32[4,20,512]{2,1,0:T(8,128)S(1)} copy(f32[4,20,512]{2,0,1:T(4,128)} %param.15) | data formatting | bytes 327680 | tf_op args[5]
  1.6 0.0 copy-done.7
  1.6 0.0 copy-done.8
  1.7 0.0 copy-start
  1.7 1.0 %copy-done = bf16[512,512]{1,0:T(8,128)(2,1)S(1)} copy-done((bf16[512,512]{1,0:T(8,128)(2,1)S(1)}, bf16[512,512]{1,0:T(8,128)(2,1)}, u32[]{:S(2)}) %copy-start) | copy-done | bytes 524312
  2.7 0.0 copy-start.1
  2.7 1.0 %copy-done.1 = bf16[512,512]{1,0:T(8,128)(2,1)S(1)} copy-done((bf16[512,512]{1,0:T(8,128)(2,1)S(1)}, bf16[512,512]{1,0:T(8,128)(2,1)}, u32[]{:S(2)}) %copy-start.1) | copy-done | bytes 524312
  3.7 0.0 copy-start.2
  3.7 1.0 %copy-done.2 = bf16[512,512]{1,0:T(8,128)(2,1)S(1)} copy-done((bf16[512,512]{1,0:T(8,128)(2,1)S(1)}, bf16[512,512]{1,0:T(8,128)(2,1)}, u32[]{:S(2)}) %copy-start.2) | copy-done | bytes 524312
  4.8 0.0 copy-start.3
  4.8 1.0 %copy-done.3 = bf16[512,512]{1,0:T(8,128)(2,1)S(1)} copy-done((bf16[512,512]{1,0:T(8,128)(2,1)S(1)}, bf16[512,512]{1,0:T(8,128)(2,1)}, u32[]{:S(2)}) %copy-start.3) | copy-done | bytes 524312
  5.8 0.0 copy-start.4
  5.8 1.0 %copy-done.4 = bf16[512,512]{1,0:T(8,128)(2,1)S(1)} copy-done((bf16[512,512]{1,0:T(8,128)(2,1)S(1)}, bf16[512,512]{1,0:T(8,128)(2,1)}, u32[]{:S(2)}) %copy-start.4) | copy-done | bytes 524312
  6.9 0.0 copy-start.5
  6.9 1.0 %copy-done.5 = bf16[512,512]{1,0:T(8,128)(2,1)S(1)} copy-done((bf16[512,512]{1,0:T(8,128)(2,1)S(1)}, bf16[512,512]{1,0:T(8,128)(2,1)}, u32[]{:S(2)}) %copy-start.5) | copy-done | bytes 524312
  7.9 0.0 copy-start.6
  7.9 1.0 %copy-done.6 = bf16[512,512]{1,0:T(8,128)(2,1)S(1)} copy-done((bf16[512,512]{1,0:T(8,128)(2,1)S(1)}, bf16[512,512]{1,0:T(8,128)(2,1)}, u32[]{:S(2)}) %copy-start.6) | copy-done | bytes 524312
  9.0 59.6 %shard_map.113 = (bf16[512,512]{1,0:T(8,128)(2,1)S(1)}, bf16[512,512]{1,0:T(8,128)(2,1)S(1)}) custom-call(bf16[512,512]{1,0:T(8,128)(2,1)S(1)} %copy-done, bf16[512,512]{1,0:T(8,128)(2,1)S(1)} %copy-done.1, bf16[512,512]{1,0:T(8,128)(2,1)S(1)} %copy-done.2, bf16[512,512]{1,0:T(8,128)(2,1)S(1)} %copy-done.3, f32[4,512]{1,0:T(4,128)S(1)} %copy-done.7, ...), custom_call_target="tpu_custom_call" | custom-call | flops 3000000000 | bytes 5000000 | tf_op jit(solution)/shard_map/pallas_call | solution.py:612
  68.6 0.8 %copy.15 = bf16[512,512]{1,0:T(8,128)(2,1)} copy(bf16[512,512]{1,0:T(8,128)(2,1)S(1)} %get-tuple-element.4) | data formatting | bytes 1048576
  69.4 0.8 %copy.16 = bf16[512,512]{1,0:T(8,128)(2,1)} copy(bf16[512,512]{1,0:T(8,128)(2,1)S(1)} %get-tuple-element.5) | data formatting | bytes 1048576
Async XLA Ops:
  0.6 1.0 %copy-start.7 = (f32[4,512]{1,0:T(4,128)S(1)}, f32[4,512]{1,0:T(4,128)}, u32[]{:S(2)}) copy-start(f32[4,512]{1,0:T(4,128)} %ld_ref.1) | copy-start | bytes 24580
  0.6 1.0 %copy-start.8 = (f32[512]{0:T(512)S(1)}, f32[512]{0:T(512)}, u32[]{:S(2)}) copy-start(f32[512]{0:T(512)} %param.16) | copy-start | bytes 6148
  1.7 1.0 %copy-start = (bf16[512,512]{1,0:T(8,128)(2,1)S(1)}, bf16[512,512]{1,0:T(8,128)(2,1)}, u32[]{:S(2)}) copy-start(bf16[512,512]{1,0:T(8,128)(2,1)} %sq_hbm.1) | copy-start | bytes 1572868
  2.7 1.0 %copy-start.1 = (bf16[512,512]{1,0:T(8,128)(2,1)S(1)}, bf16[512,512]{1,0:T(8,128)(2,1)}, u32[]{:S(2)}) copy-start(bf16[512,512]{1,0:T(8,128)(2,1)} %sk_hbm.1) | copy-start | bytes 1572868
  3.7 1.0 %copy-start.2 = (bf16[512,512]{1,0:T(8,128)(2,1)S(1)}, bf16[512,512]{1,0:T(8,128)(2,1)}, u32[]{:S(2)}) copy-start(bf16[512,512]{1,0:T(8,128)(2,1)} %sv_hbm.1) | copy-start | bytes 1572868
  4.8 1.0 %copy-start.3 = (bf16[512,512]{1,0:T(8,128)(2,1)S(1)}, bf16[512,512]{1,0:T(8,128)(2,1)}, u32[]{:S(2)}) copy-start(bf16[512,512]{1,0:T(8,128)(2,1)} %sg_hbm.1) | copy-start | bytes 1572868
  5.8 1.0 %copy-start.4 = (bf16[512,512]{1,0:T(8,128)(2,1)S(1)}, bf16[512,512]{1,0:T(8,128)(2,1)}, u32[]{:S(2)}) copy-start(bf16[512,512]{1,0:T(8,128)(2,1)} %aq_hbm.1) | copy-start | bytes 1572868
  6.9 1.0 %copy-start.5 = (bf16[512,512]{1,0:T(8,128)(2,1)S(1)}, bf16[512,512]{1,0:T(8,128)(2,1)}, u32[]{:S(2)}) copy-start(bf16[512,512]{1,0:T(8,128)(2,1)} %ak_hbm.1) | copy-start | bytes 1572868
  7.9 1.0 %copy-start.6 = (bf16[512,512]{1,0:T(8,128)(2,1)S(1)}, bf16[512,512]{1,0:T(8,128)(2,1)}, u32[]{:S(2)}) copy-start(bf16[512,512]{1,0:T(8,128)(2,1)} %av_hbm.1) | copy-start | bytes 1572868

commit v2 on v1

--- a/solution.py
+++ b/solution.py
@@ -31,7 +31,7 @@
     sv_hbm,
     sg_hbm,
     ld_ref,
-    lg_ref,
+    lg_hbm,
     gain_ref,
     aq_hbm,
     ak_hbm,
@@ -46,10 +46,12 @@
     kbuf,
     vbuf,
     obuf,
+    lgbuf,
     grow,
     gcol,
     mixed,
     gated,
+    reached,
     mout,
     ssend,
     srecv,
@@ -99,6 +101,8 @@
         pltpu.make_async_copy(src, dst, loc_sem.at[i])
         for i, (src, dst) in enumerate(((sk_hbm, sk), (sv_hbm, sv), (sq_hbm, sq), (sg_hbm, sg)))
     ]
+    gates_in = pltpu.make_async_copy(lg_hbm, lgbuf, loc_sem.at[7])
+    gates_in.start()
     for c in state_in:
         c.start()
     att = ((ak_hbm, kbuf, 3), (av_hbm, vbuf, 3), (aq_hbm, qbuf, 0))
@@ -130,7 +134,6 @@
         )
     for d in range(1, hn):
         pl.semaphore_signal(barrier, inc=1, device_id={"head": (mh + d) % hn}, device_id_type=MESH)
-    pl.semaphore_wait(barrier, ROW - 1 + zn - 1 + hn - 1)
 
     def x_copy(t, d):
         src, dst, base = att[t]
@@ -252,15 +255,6 @@
     def o_local(j):
         return pltpu.make_async_copy(obuf.at[j], ao_hbm.at[:, cols(x)], out_sem.at[1])
 
-    for d in (1, 3, 2):
-        x_copy(0, d).start()
-    own_halo = (x >= 1) & (z < zn - 1)
-
-    @pl.when(own_halo)
-    def _():
-        halo_own(0).start()
-        halo_own(1).start()
-
     lane = lax.broadcasted_iota(jnp.int32, (8, tok), 1)
     cum = jnp.concatenate([ld_ref[...], jnp.zeros((8 - ROW, tok), F32)], axis=0)
     shift = 1
@@ -270,8 +264,9 @@
     last = cum[:, tok - 1 : tok]
     tail = jnp.exp(last - cum)
     reach = jnp.exp(cum)
+    gates_in.wait()
     for h in range(ROW):
-        grow[h, 0:20, :] = lg_ref[h]
+        grow[h, 0:20, :] = lgbuf[:, h, :]
         grow[h, 20:21, :] = cum[h : h + 1]
         grow[h, 21:22, :] = tail[h : h + 1]
         grow[h, 22:23, :] = reach[h : h + 1]
@@ -280,6 +275,17 @@
         tsend[h] = jnp.broadcast_to(last[h : h + 1], (8, 128))
         gcol[h] = grow[h].T
 
+    pl.semaphore_wait(barrier, ROW - 1 + zn - 1 + hn - 1)
+
+    for d in (1, 3):
+        x_copy(0, d).start()
+    own_halo = (x >= 1) & (z < zn - 1)
+
+    @pl.when(own_halo)
+    def _():
+        halo_own(0).start()
+        halo_own(1).start()
+
     state_in[0].wait()
     state_in[1].wait()
 
@@ -293,9 +299,8 @@
     for d in (1, 3, 2):
         for c in s_copies(d):
             c.start()
-    for t in (1, 2):
-        for d in (1, 3, 2):
-            x_copy(t, d).start()
+    for t, d in ((1, 1), (1, 3), (0, 2), (1, 2), (2, 1), (2, 3), (2, 2)):
+        x_copy(t, d).start()
     srecv[x] = ssend[x]
     trecv[x] = tsend[x]
 
@@ -303,6 +308,13 @@
     state_in[3].wait()
     row_i = lax.broadcasted_iota(jnp.int32, (chunk, chunk), 0)
     col_i = lax.broadcasted_iota(jnp.int32, (chunk, chunk), 1)
+
+    def relay(t, d):
+        x_wait(t, d)
+
+        @pl.when(relay_if(d))
+        def _():
+            halo_relay(t, d).start()
 
     apart = row_i ^ col_i
 
@@ -334,7 +346,23 @@
             )
         return 0
 
-    lax.fori_loop(0, ROW, inside, 0)
+    lax.fori_loop(0, ROW // 2, inside, 0)
+    relay(0, 1)
+    relay(0, 3)
+    lax.fori_loop(ROW // 2, ROW, inside, 0)
+
+    def reaching(h, _):
+        hc = cols(h)
+        for i in range(chunks):
+            rows = pl.ds(i * chunk, chunk)
+            g = gcol[h, rows, :]
+            qf = sq[rows, hc].astype(F32) * g[:, 22:23]
+            near = jnp.where(x == 2, g[:, 11:12], g[:, 10:11])
+            for m, gate in enumerate((g[:, 12:13], g[:, 13:14], g[:, 14:15], near, g[:, 11:12])):
+                reached[h, rows, m * hd : (m + 1) * hd] = (qf * gate).astype(BF16)
+            v = sg[rows, hc].astype(F32)
+            gated[rows, hc] = v / (1.0 + jnp.exp(-v))
+        return 0
 
     for d in range(1, ROW):
         p = (x + ROW - d) % ROW
@@ -362,65 +390,10 @@
             for c in r_copies(d):
                 c.start()
 
-    for c in own_in:
-        c.wait()
-    for d in (1, 3, 2):
-        for t in (0, 1):
-            x_wait(t, d)
-
-            @pl.when(relay_if(d))
-            def _():
-                halo_relay(t, d).start()
-
-    for d in (1, 3, 2):
-        x_wait(2, d)
-
-    kappa = math.log2(math.e) / math.sqrt(hd)
-    qrows = 256
-    absent = jnp.where(z == 0, NEG, 0.0).astype(F32)
-
-    def attend(j):
-        def body(i, _):
-            first = pl.multiple_of(i * qrows, qrows)
-            q = qbuf[j, pl.ds(first, qrows), :]
-            logits = []
-            for s in range(ROW):
-                part = nt_dot(q, kbuf[j + s])
-                if j + s < 3:
-                    part = part + absent
-                if s == ROW - 1:
-                    r = lax.broadcasted_iota(jnp.int32, (qrows, tok), 0) + first
-                    c = lax.broadcasted_iota(jnp.int32, (qrows, tok), 1)
-                    part = jnp.where(r >= c, part, NEG)
-                logits.append(part)
-            top = jnp.maximum(
-                jnp.maximum(logits[0], logits[1]), jnp.maximum(logits[2], logits[3])
-            )
-            top = jnp.max(top, axis=1, keepdims=True)
-            weights = [jnp.exp2((part - top) * kappa) for part in logits]
-            total = jnp.sum(
-                (weights[0] + weights[1]) + (weights[2] + weights[3]), axis=1, keepdims=True
-            )
-            out = None
-            for s in range(ROW):
-                term = jnp.dot(
-                    weights[s].astype(BF16), vbuf[j + s], preferred_element_type=F32
-                )
-                out = term if out is None else out + term
-            obuf[j, pl.ds(first, qrows), :] = (out / total).astype(BF16)
-            return 0
-
-        lax.fori_loop(0, tok // qrows, body, 0)
-
-        @pl.when(x != j)
-        def _():
-            o_copy(j).start()
-
-        @pl.when(x == j)
-        def _():
-            o_local(j).start()
-
-    attend(3)
+    lax.fori_loop(0, ROW, reaching, 0)
+
+    for t, d in ((1, 1), (1, 3), (0, 2), (1, 2)):
+        relay(t, d)
 
     for d in range(1, zn):
 
@@ -467,14 +440,73 @@
     def _():
         lrecv[x, 4] = lsend[0, 4]
 
-    def halos(slot):
-        @pl.when(z > 0)
-        def _():
-            for t in (0, 1):
-                halo_wait(t, slot)
-
-    halos(2)
-    attend(2)
+    for c in own_in:
+        c.wait()
+
+    kappa = math.log2(math.e) / math.sqrt(hd)
+    qrows = 256
+    absent = jnp.where(z == 0, NEG, 0.0).astype(F32)
+
+    def attend(j):
+        def body(i, _):
+            first = pl.multiple_of(i * qrows, qrows)
+            q = qbuf[j, pl.ds(first, qrows), :]
+            logits = []
+            for s in range(ROW):
+                part = nt_dot(q, kbuf[j + s])
+                if s < 3:
+                    part = part + jnp.where(j + s < 3, absent, 0.0)
+                if s == ROW - 1:
+                    r = lax.broadcasted_iota(jnp.int32, (qrows, tok), 0) + first
+                    c = lax.broadcasted_iota(jnp.int32, (qrows, tok), 1)
+                    part = jnp.where(r >= c, part, NEG)
+                logits.append(part)
+            top = jnp.maximum(
+                jnp.maximum(logits[0], logits[1]), jnp.maximum(logits[2], logits[3])
+            )
+            top = jnp.max(top, axis=1, keepdims=True)
+            weights = [jnp.exp2((part - top) * kappa) for part in logits]
+            total = jnp.sum(
+                (weights[0] + weights[1]) + (weights[2] + weights[3]), axis=1, keepdims=True
+            )
+            out = None
+            for s in range(ROW):
+                term = jnp.dot(
+                    weights[s].astype(BF16), vbuf[j + s], preferred_element_type=F32
+                )
+                out = term if out is None else out + term
+            obuf[j, pl.ds(first, qrows), :] = (out / total).astype(BF16)
+            return 0
+
+        lax.fori_loop(0, tok // qrows, body, 0)
+
+    def turn(k):
+        if k < ROW - 1:
+            return jnp.where(ROW - 1 - k > x, ROW - 1 - k, ROW - 2 - k)
+        return x
+
+    def step(k):
+        j = turn(k)
+        done = turn(k - 1) if k > 0 else ROW - 1
+        for slot in (2, 1, 0):
+
+            @pl.when((z > 0) & (slot >= j) & (slot < done))
+            def _():
+                for t in (0, 1):
+                    halo_wait(t, slot)
+
+        if k < ROW - 1:
+            d = (x + ROW - j) % ROW
+            x_wait(2, d)
+        attend(j)
+        if k < ROW - 1:
+            o_copy(j).start()
+        else:
+            o_local(j).start()
+
+    step(0)
+
+    step(1)
 
     for d in range(1, ROW):
         p = (x + ROW - d) % ROW
@@ -501,21 +533,11 @@
     def across(h, acc):
         hc = cols(h)
         squares = []
+        states = lrecv[h].reshape(5 * hd, hd)
         for i in range(chunks):
             rows = pl.ds(i * chunk, chunk)
-            g = gcol[h, rows, :]
-            qf = sq[rows, hc].astype(F32) * g[:, 22:23]
-            near = jnp.where(x == 2, g[:, 11:12], g[:, 10:11])
-            low = jnp.concatenate(
-                [
-                    (qf * gate).astype(BF16)
-                    for gate in (g[:, 12:13], g[:, 13:14], g[:, 14:15], near, g[:, 11:12])
-                ],
-                axis=1,
-            )
-            far = jnp.dot(low, lrecv[h].reshape(5 * hd, hd), preferred_element_type=F32)
-            v = sg[rows, hc].astype(F32)
-            out = (mixed[h, rows, :] + far) * (v / (1.0 + jnp.exp(-v)))
+            far = jnp.dot(reached[h, rows, :], states, preferred_element_type=F32)
+            out = (mixed[h, rows, :] + far) * gated[rows, hc]
             gated[rows, hc] = out
             squares.append(out * out)
         return tuple(a + s for a, s in zip(acc, squares))
@@ -529,10 +551,8 @@
     for d in range(1, hn):
         n_copy(d).start()
 
-    halos(1)
-    attend(1)
-    halos(0)
-    attend(0)
+    step(2)
+    step(3)
 
     total = nsend[...]
     for d in range(1, hn):
@@ -599,6 +619,10 @@
     mix_out.wait()
 
 
+def hbm(*arrays):
+    return [pltpu.with_memory_space_constraint(a, pltpu.HBM) for a in arrays]
+
+
 def shards(zn, hn, sq, sk, sv, sg, ld, lg, gain, aq, ak, av):
     tok = sq.shape[0]
     heads = ld.shape[0]
@@ -606,13 +630,13 @@
     wide = heads * hd
     dma = pltpu.SemaphoreType.DMA
     vm = pltpu.VMEM
-    anywhere = pl.BlockSpec(memory_space=pl.ANY)
+    anywhere = pl.BlockSpec(memory_space=pltpu.HBM)
     here = pl.BlockSpec(memory_space=pltpu.VMEM)
     out = jax.ShapeDtypeStruct((tok, wide), BF16)
     return pl.pallas_call(
         functools.partial(kernel, zn, hn),
         out_shape=(out, out),
-        in_specs=[anywhere] * 4 + [here] * 3 + [anywhere] * 3,
+        in_specs=[anywhere] * 4 + [here, anywhere, here] + [anywhere] * 3,
         out_specs=(anywhere, anywhere),
         scratch_shapes=[
             vm((tok, wide), BF16),
@@ -623,10 +647,12 @@
             vm((7, tok, hd), BF16),
             vm((7, tok, hd), BF16),
             vm((4, tok, hd), BF16),
+            vm((lg.shape[1], heads, tok), F32),
             vm((heads, 32, tok), F32),
             vm((heads, tok, 32), F32),
             vm((heads, tok, hd), F32),
             vm((tok, wide), F32),
+            vm((heads, tok, 5 * hd), BF16),
             vm((tok, wide), BF16),
             vm((4, hd, hd), BF16),
             vm((4, hd, hd), BF16),
@@ -640,7 +666,7 @@
             vm((4, 5, hd, hd), BF16),
             vm((8, 128), F32),
             vm((max(hn - 1, 1), 8, 128), F32),
-            dma((7,)),
+            dma((8,)),
             dma((3, 3)),
             dma((3, 3)),
             dma((2, 4)),
@@ -663,7 +689,7 @@
         cost_estimate=pl.CostEstimate(
             flops=3_000_000_000, bytes_accessed=5_000_000, transcendentals=5_000_000
         ),
-    )(sq, sk, sv, sg, ld, lg, gain.reshape(1, wide), aq, ak, av)
+    )(*hbm(sq, sk, sv, sg), ld, *hbm(jnp.transpose(lg, (1, 0, 2))), gain.reshape(1, wide), *hbm(aq, ak, av))
 
 
 def solution(mesh):

time: 70.8 us -> 52.3 us (0.74)
  Pallas kernels: 59.6 us -> 48.6 us
  local copies, waits for them, and re-layouts: 9.86 us -> 2.96 us
    pallas_call x1, Pallas kernels: 59.6 us -> 48.6 us  [shards(): pl.pallas_call(functools.partial(kernel, zn, hn), out_shape=(out, out), i...]
    unnamed x21 -> x6, local copies, waits for them, and re-layouts: 9.86 us -> 2.96 us
where the time goes in v2:
time: 52.3 us; the launch traced here: 52.2 us
  Pallas kernels  48.6 us (93%)
  local copies, waits for them, and re-layouts  2.96 us (6%)
  between operations  0.65 us (1%)
    pallas_call x1, Pallas kernels, shards(): pl.pallas_call(functools.partial(kernel, zn, hn), out_shape=(out, out), i...  48.6 us
    unnamed x6, local copies, waits for them, and re-layouts  2.96 us

profile of v2, /device:TPU:16, one launch (start us, length us, event | category | flops | bytes accessed | tf_op | source)
XLA Modules:
  0.0 52.2 jit_solution(12234397138773656689)
XLA Ops:
  0.6 0.0 copy-start.1
  0.6 0.7 %copy-done.1 = f32[512]{0:T(512)S(1)} copy-done((f32[512]{0:T(512)S(1)}, f32[512]{0:T(512)}, u32[]{:S(2)}) %copy-start.1) | copy-done | bytes 2072
  1.3 0.0 copy-start
  1.3 0.7 %copy-done = f32[4,512]{1,0:T(4,128)S(1)} copy-done((f32[4,512]{1,0:T(4,128)S(1)}, f32[4,512]{1,0:T(4,128)}, u32[]{:S(2)}) %copy-start) | copy-done | bytes 8216
  2.0 48.6 %shard_map.113 = (bf16[512,512]{1,0:T(8,128)(2,1)S(1)}, bf16[512,512]{1,0:T(8,128)(2,1)S(1)}) custom-call(bf16[512,512]{1,0:T(8,128)(2,1)} %sq_hbm.1, bf16[512,512]{1,0:T(8,128)(2,1)} %sk_hbm.1, bf16[512,512]{1,0:T(8,128)(2,1)} %sv_hbm.1, bf16[512,512]{1,0:T(8,128)(2,1)} %sg_hbm.1, f32[4,512]{1,0:T(4,128)S(1)} %copy-done, f32[20,4,512]{2,1,0:T(4,128)} %bitcast.3, ...), custom_call_target="tpu_custom_call" | custom-call | flops 3000000000 | bytes 5000000 | tf_op jit(solution)/shard_map/pallas_call | solution.py:636
  50.6 0.8 %copy.14 = bf16[512,512]{1,0:T(8,128)(2,1)} copy(bf16[512,512]{1,0:T(8,128)(2,1)S(1)} %get-tuple-element.4) | data formatting | bytes 1048576
  51.4 0.8 %copy.15 = bf16[512,512]{1,0:T(8,128)(2,1)} copy(bf16[512,512]{1,0:T(8,128)(2,1)S(1)} %get-tuple-element.5) | data formatting | bytes 1048576
Async XLA Ops:
  0.6 0.7 %copy-start.1 = (f32[512]{0:T(512)S(1)}, f32[512]{0:T(512)}, u32[]{:S(2)}) copy-start(f32[512]{0:T(512)} %param.16) | copy-start | bytes 6148
  1.3 0.7 %copy-start = (f32[4,512]{1,0:T(4,128)S(1)}, f32[4,512]{1,0:T(4,128)}, u32[]{:S(2)}) copy-start(f32[4,512]{1,0:T(4,128)} %ld_ref.1) | copy-start | bytes 24580

commit v3 on v2

--- a/solution.py
+++ b/solution.py
@@ -30,9 +30,9 @@
     sk_hbm,
     sv_hbm,
     sg_hbm,
-    ld_ref,
+    ld_hbm,
     lg_hbm,
-    gain_ref,
+    gain_hbm,
     aq_hbm,
     ak_hbm,
     av_hbm,
@@ -47,6 +47,8 @@
     vbuf,
     obuf,
     lgbuf,
+    ldbuf,
+    gainbuf,
     grow,
     gcol,
     mixed,
@@ -81,6 +83,7 @@
     o_send,
     o_recv,
     out_sem,
+    ready,
 ):
     me = lax.axis_index("ctx")
     mh = lax.axis_index("head")
@@ -97,14 +100,44 @@
     def cols(h):
         return pl.ds(pl.multiple_of(h * hd, hd), hd)
 
+    rrecv[...] = jnp.zeros_like(rrecv)
+    trrecv[...] = jnp.zeros_like(trrecv)
+
+    @pl.when(x != 3)
+    def _():
+        lrecv[:, 4] = jnp.zeros_like(lrecv[:, 4])
+
+    @pl.when(z == 0)
+    def _():
+        kbuf[0:3] = jnp.zeros((3, tok, hd), BF16)
+        vbuf[0:3] = jnp.zeros((3, tok, hd), BF16)
+
+    barrier = pltpu.get_barrier_semaphore()
+    for d in range(1, ROW):
+        pl.semaphore_signal(barrier, inc=1, device_id={"ctx": rowdev(d)}, device_id_type=MESH)
+    for d in range(1, zn):
+
+        @pl.when(z + d < zn)
+        def _():
+            pl.semaphore_signal(
+                barrier, inc=1, device_id={"ctx": (z + d) * ROW + x}, device_id_type=MESH
+            )
+
+    for d in range(1, hn):
+        pl.semaphore_signal(barrier, inc=1, device_id={"head": (mh + d) % hn}, device_id_type=MESH)
+
     state_in = [
         pltpu.make_async_copy(src, dst, loc_sem.at[i])
         for i, (src, dst) in enumerate(((sk_hbm, sk), (sv_hbm, sv), (sq_hbm, sq), (sg_hbm, sg)))
     ]
     gates_in = pltpu.make_async_copy(lg_hbm, lgbuf, loc_sem.at[7])
+    decay_in = pltpu.make_async_copy(ld_hbm, ldbuf, loc_sem.at[8])
+    gain_in = pltpu.make_async_copy(gain_hbm, gainbuf, loc_sem.at[9])
+    decay_in.start()
     gates_in.start()
     for c in state_in:
         c.start()
+    gain_in.start()
     att = ((ak_hbm, kbuf, 3), (av_hbm, vbuf, 3), (aq_hbm, qbuf, 0))
     own_in = [
         pltpu.make_async_copy(src.at[:, cols(x)], dst.at[base + x], loc_sem.at[4 + i])
@@ -112,28 +145,6 @@
     ]
     for c in own_in:
         c.start()
-
-    rrecv[...] = jnp.zeros_like(rrecv)
-    trrecv[...] = jnp.zeros_like(trrecv)
-
-    @pl.when(x != 3)
-    def _():
-        lrecv[:, 4] = jnp.zeros_like(lrecv[:, 4])
-
-    @pl.when(z == 0)
-    def _():
-        kbuf[0:3] = jnp.zeros((3, tok, hd), BF16)
-        vbuf[0:3] = jnp.zeros((3, tok, hd), BF16)
-
-    barrier = pltpu.get_barrier_semaphore()
-    for d in range(1, ROW):
-        pl.semaphore_signal(barrier, inc=1, device_id={"ctx": rowdev(d)}, device_id_type=MESH)
-    for d in range(1, zn):
-        pl.semaphore_signal(
-            barrier, inc=1, device_id={"ctx": ((z + d) % zn) * ROW + x}, device_id_type=MESH
-        )
-    for d in range(1, hn):
-        pl.semaphore_signal(barrier, inc=1, device_id={"head": (mh + d) % hn}, device_id_type=MESH)
 
     def x_copy(t, d):
         src, dst, base = att[t]
@@ -255,8 +266,21 @@
     def o_local(j):
         return pltpu.make_async_copy(obuf.at[j], ao_hbm.at[:, cols(x)], out_sem.at[1])
 
+    pl.semaphore_wait(barrier, ROW - 1 + z + hn - 1)
+    for d in range(1, zn):
+
+        @pl.when(z - d >= 0)
+        def _():
+            pl.semaphore_signal(
+                ready.at[d - 1], inc=1, device_id={"ctx": (z - d) * ROW + x}, device_id_type=MESH
+            )
+
+    for d in (1, 3):
+        x_copy(0, d).start()
+
+    decay_in.wait()
     lane = lax.broadcasted_iota(jnp.int32, (8, tok), 1)
-    cum = jnp.concatenate([ld_ref[...], jnp.zeros((8 - ROW, tok), F32)], axis=0)
+    cum = jnp.concatenate([ldbuf[...], jnp.zeros((8 - ROW, tok), F32)], axis=0)
     shift = 1
     while shift < tok:
         cum = cum + jnp.where(lane >= shift, pltpu.roll(cum, shift, axis=1), 0.0)
@@ -275,17 +299,6 @@
         tsend[h] = jnp.broadcast_to(last[h : h + 1], (8, 128))
         gcol[h] = grow[h].T
 
-    pl.semaphore_wait(barrier, ROW - 1 + zn - 1 + hn - 1)
-
-    for d in (1, 3):
-        x_copy(0, d).start()
-    own_halo = (x >= 1) & (z < zn - 1)
-
-    @pl.when(own_halo)
-    def _():
-        halo_own(0).start()
-        halo_own(1).start()
-
     state_in[0].wait()
     state_in[1].wait()
 
@@ -301,6 +314,17 @@
             c.start()
     for t, d in ((1, 1), (1, 3), (0, 2), (1, 2), (2, 1), (2, 3), (2, 2)):
         x_copy(t, d).start()
+    own_halo = (x >= 1) & (z < zn - 1)
+
+    @pl.when(z < zn - 1)
+    def _():
+        pl.semaphore_wait(ready.at[0], 1)
+
+    @pl.when(own_halo)
+    def _():
+        halo_own(0).start()
+        halo_own(1).start()
+
     srecv[x] = ssend[x]
     trecv[x] = tsend[x]
 
@@ -387,6 +411,8 @@
 
         @pl.when(z + d < zn)
         def _():
+            if d > 1:
+                pl.semaphore_wait(ready.at[d - 1], 1)
             for c in r_copies(d):
                 c.start()
 
@@ -480,14 +506,13 @@
 
         lax.fori_loop(0, tok // qrows, body, 0)
 
-    def turn(k):
-        if k < ROW - 1:
-            return jnp.where(ROW - 1 - k > x, ROW - 1 - k, ROW - 2 - k)
-        return x
+    turns = (ROW - 1 - x, (x + 2) % ROW, x + 1 - 2 * (x % 2), x)
 
     def step(k):
-        j = turn(k)
-        done = turn(k - 1) if k > 0 else ROW - 1
+        j = turns[k]
+        done = ROW - 1
+        for earlier in turns[:k]:
+            done = jnp.minimum(done, earlier)
         for slot in (2, 1, 0):
 
             @pl.when((z > 0) & (slot >= j) & (slot < done))
@@ -507,6 +532,8 @@
     step(0)
 
     step(1)
+
+    step(2)
 
     for d in range(1, ROW):
         p = (x + ROW - d) % ROW
@@ -551,20 +578,20 @@
     for d in range(1, hn):
         n_copy(d).start()
 
-    step(2)
     step(3)
 
     total = nsend[...]
     for d in range(1, hn):
         n_copy(d).wait_recv()
         total = total + nrecv[d - 1]
+    gain_in.wait()
     scale = lax.rsqrt(total / (hn * ROW * hd) + 1e-05)
     for i in range(chunks):
         rows = pl.ds(i * chunk, chunk)
         scale_col = jnp.broadcast_to(scale[i : i + 1], (chunk, chunk)).T
         for h in range(ROW):
             hs = slice(h * hd, (h + 1) * hd)
-            mout[rows, hs] = (gated[rows, hs] * scale_col * gain_ref[:, hs]).astype(BF16)
+            mout[rows, hs] = (gated[rows, hs] * scale_col * gainbuf[:, hs]).astype(BF16)
     mix_out = pltpu.make_async_copy(mout, mo_hbm, out_sem.at[0])
     mix_out.start()
 
@@ -631,12 +658,11 @@
     dma = pltpu.SemaphoreType.DMA
     vm = pltpu.VMEM
     anywhere = pl.BlockSpec(memory_space=pltpu.HBM)
-    here = pl.BlockSpec(memory_space=pltpu.VMEM)
     out = jax.ShapeDtypeStruct((tok, wide), BF16)
     return pl.pallas_call(
         functools.partial(kernel, zn, hn),
         out_shape=(out, out),
-        in_specs=[anywhere] * 4 + [here, anywhere, here] + [anywhere] * 3,
+        in_specs=[anywhere] * 10,
         out_specs=(anywhere, anywhere),
         scratch_shapes=[
             vm((tok, wide), BF16),
@@ -648,6 +674,8 @@
             vm((7, tok, hd), BF16),
             vm((4, tok, hd), BF16),
             vm((lg.shape[1], heads, tok), F32),
+            vm((heads, tok), F32),
+            vm((1, wide), F32),
             vm((heads, 32, tok), F32),
             vm((heads, tok, 32), F32),
             vm((heads, tok, hd), F32),
@@ -666,7 +694,7 @@
             vm((4, 5, hd, hd), BF16),
             vm((8, 128), F32),
             vm((max(hn - 1, 1), 8, 128), F32),
-            dma((8,)),
+            dma((10,)),
             dma((3, 3)),
             dma((3, 3)),
             dma((2, 4)),
@@ -682,6 +710,7 @@
             dma((4,)),
             dma((4,)),
             dma((2,)),
+            pltpu.SemaphoreType.REGULAR((max(zn - 1, 1),)),
         ],
         compiler_params=pltpu.CompilerParams(
             collective_id=0, has_side_effects=True, vmem_limit_bytes=48 * 1024 * 1024
@@ -689,7 +718,7 @@
         cost_estimate=pl.CostEstimate(
             flops=3_000_000_000, bytes_accessed=5_000_000, transcendentals=5_000_000
         ),
-    )(*hbm(sq, sk, sv, sg), ld, *hbm(jnp.transpose(lg, (1, 0, 2))), gain.reshape(1, wide), *hbm(aq, ak, av))
+    )(*hbm(sq, sk, sv, sg, ld, jnp.transpose(lg, (1, 0, 2)), gain.reshape(1, wide), aq, ak, av))
 
 
 def solution(mesh):

time: 52.3 us -> 46.3 us (0.89)
  the two profiles are of different devices: /device:TPU:16 before, /device:TPU:131 now
where the time goes in v3:
time: 46.3 us; the launch traced here: 46.2 us
  Pallas kernels  44 us (95%)
  local copies, waits for them, and re-layouts  1.59 us (3%)
  between operations  0.64 us (1%)
    pallas_call x1, Pallas kernels, shards(): pl.pallas_call(functools.partial(kernel, zn, hn), out_shape=(out, out), i...  44 us
    unnamed x2, local copies, waits for them, and re-layouts  1.59 us

profile of v3, /device:TPU:131, one launch (start us, length us, event | category | flops | bytes accessed | tf_op | source)
XLA Modules:
  0.0 46.2 jit_solution(6940868982949188101)
XLA Ops:
  0.6 44.0 %shard_map.113 = (bf16[512,512]{1,0:T(8,128)(2,1)S(1)}, bf16[512,512]{1,0:T(8,128)(2,1)S(1)}) custom-call(bf16[512,512]{1,0:T(8,128)(2,1)} %sq_hbm.1, bf16[512,512]{1,0:T(8,128)(2,1)} %sk_hbm.1, bf16[512,512]{1,0:T(8,128)(2,1)} %sv_hbm.1, bf16[512,512]{1,0:T(8,128)(2,1)} %sg_hbm.1, f32[4,512]{1,0:T(4,128)} %ld_hbm.1, f32[20,4,512]{2,1,0:T(4,128)} %bitcast.2, ...), custom_call_target="tpu_custom_call" | custom-call | flops 3000000000 | bytes 5000000 | tf_op jit(solution)/shard_map/pallas_call | solution.py:662
  44.6 0.8 %copy.14 = bf16[512,512]{1,0:T(8,128)(2,1)} copy(bf16[512,512]{1,0:T(8,128)(2,1)S(1)} %get-tuple-element.4) | data formatting | bytes 1048576
  45.4 0.8 %copy.15 = bf16[512,512]{1,0:T(8,128)(2,1)} copy(bf16[512,512]{1,0:T(8,128)(2,1)S(1)} %get-tuple-element.5) | data formatting | bytes 1048576

commit v4 on v3

--- a/solution.py
+++ b/solution.py
@@ -63,6 +63,8 @@
     rrecv,
     trsend,
     trrecv,
+    asend,
+    arecv,
     lsend,
     lrecv,
     nsend,
@@ -84,6 +86,8 @@
     o_recv,
     out_sem,
     ready,
+    a_send,
+    a_recv,
 ):
     me = lax.axis_index("ctx")
     mh = lax.axis_index("head")
@@ -100,12 +104,22 @@
     def cols(h):
         return pl.ds(pl.multiple_of(h * hd, hd), hd)
 
+    zl = z % 4
+
+    def sends_to(d):
+        return ((zl + d < 4) | (z == 3)) & (z + d < zn)
+
+    def hears_from(d):
+        return (zl >= d) | (z - d == 3)
+
+    reaches = range(1, min(zn, 5))
+    group = range(1, min(zn, 4))
+
     rrecv[...] = jnp.zeros_like(rrecv)
+    arecv[...] = jnp.zeros_like(arecv)
     trrecv[...] = jnp.zeros_like(trrecv)
 
-    @pl.when(x != 3)
-    def _():
-        lrecv[:, 4] = jnp.zeros_like(lrecv[:, 4])
+    lrecv[...] = jnp.zeros_like(lrecv)
 
     @pl.when(z == 0)
     def _():
@@ -115,9 +129,9 @@
     barrier = pltpu.get_barrier_semaphore()
     for d in range(1, ROW):
         pl.semaphore_signal(barrier, inc=1, device_id={"ctx": rowdev(d)}, device_id_type=MESH)
-    for d in range(1, zn):
-
-        @pl.when(z + d < zn)
+    for d in reaches:
+
+        @pl.when(sends_to(d))
         def _():
             pl.semaphore_signal(
                 barrier, inc=1, device_id={"ctx": (z + d) * ROW + x}, device_id_type=MESH
@@ -232,13 +246,27 @@
             for i, (src, dst) in enumerate(((rsend, rrecv), (trsend, trrecv)))
         ]
 
-    def l_copy(i, d):
-        part = pl.ds(0, 4) if i == 0 else pl.ds(4, 1)
+    def a_copy(d):
         return pltpu.make_async_remote_copy(
-            src_ref=lsend.at[d, part],
-            dst_ref=lrecv.at[x, part],
-            send_sem=l_send.at[i, d - 1],
-            recv_sem=l_recv.at[i, d - 1],
+            src_ref=asend,
+            dst_ref=arecv,
+            send_sem=a_send.at[d - 1],
+            recv_sem=a_recv.at[0],
+            device_id={"ctx": ((z + d) % zn) * ROW + x},
+            device_id_type=MESH,
+        )
+
+    def l_used(m, block):
+        if m < 3:
+            return z // 2**m % 2 == 1
+        return block >= 1 if m == 3 else block == 3
+
+    def l_copy(m, d, source):
+        return pltpu.make_async_remote_copy(
+            src_ref=lsend.at[d, m],
+            dst_ref=lrecv.at[source, m],
+            send_sem=l_send.at[m, d - 1],
+            recv_sem=l_recv.at[m, d - 1],
             device_id={"ctx": rowdev(d)},
             device_id_type=MESH,
         )
@@ -266,10 +294,10 @@
     def o_local(j):
         return pltpu.make_async_copy(obuf.at[j], ao_hbm.at[:, cols(x)], out_sem.at[1])
 
-    pl.semaphore_wait(barrier, ROW - 1 + z + hn - 1)
-    for d in range(1, zn):
-
-        @pl.when(z - d >= 0)
+    pl.semaphore_wait(barrier, ROW - 1 + zl + z // 4 + hn - 1)
+    for d in reaches:
+
+        @pl.when(hears_from(d))
         def _():
             pl.semaphore_signal(
                 ready.at[d - 1], inc=1, device_id={"ctx": (z - d) * ROW + x}, device_id_type=MESH
@@ -323,7 +351,6 @@
     @pl.when(own_halo)
     def _():
         halo_own(0).start()
-        halo_own(1).start()
 
     srecv[x] = ssend[x]
     trecv[x] = tsend[x]
@@ -407,58 +434,97 @@
     )
     rsend[...] = row_state.astype(BF16)
     trsend[...] = tot[0] + tot[1] + tot[2] + tot[3]
-    for d in range(1, zn):
-
-        @pl.when(z + d < zn)
-        def _():
-            if d > 1:
+    for d in reaches:
+        if d > 1:
+
+            @pl.when(sends_to(d))
+            def _():
                 pl.semaphore_wait(ready.at[d - 1], 1)
+
+    for d in group:
+
+        @pl.when(zl + d < 4)
+        def _():
             for c in r_copies(d):
                 c.start()
 
+
+    @pl.when(own_halo)
+    def _():
+        halo_own(1).start()
+
     lax.fori_loop(0, ROW, reaching, 0)
 
-    for t, d in ((1, 1), (1, 3), (0, 2), (1, 2)):
-        relay(t, d)
-
-    for d in range(1, zn):
-
-        @pl.when(z - d >= 0)
+    for d in group:
+
+        @pl.when(zl >= d)
         def _():
             for c in r_copies(d):
                 c.wait_recv()
 
-    levels = [jnp.zeros((hd, hd), F32) for _ in range(3)]
+    levels = [jnp.zeros((hd, hd), F32) for _ in range(2)]
     decay = jnp.zeros((8, 128), F32)
-    for d in range(1, zn):
-        other = z + zn - d
-        near2 = (z + zn) // 2 == other // 2
-        near4 = (z + zn) // 4 == other // 4
+    for d in group:
+        near2 = (zl + 4) // 2 == (zl + 4 - d) // 2
         w = jnp.exp(decay)[0:1]
         held = rrecv[d - 1].astype(F32)
         levels[0] = levels[0] + jnp.where(near2, w, 0.0) * held
-        levels[1] = levels[1] + jnp.where(near4 & ~near2, w, 0.0) * held
-        levels[2] = levels[2] + jnp.where(near4, 0.0, w) * held
+        levels[1] = levels[1] + jnp.where(near2, 0.0, w) * held
         decay = decay + trrecv[d - 1]
-    for d in (0, 1, 3, 2):
-        xp = (x + d) % ROW
-        before = (
+    asend[...] = (
+        (levels[0] + levels[1]) * jnp.exp(trsend[0:1]) + row_state
+    ).astype(BF16)
+    for d in reaches:
+
+        @pl.when((z == 3) & sends_to(d))
+        def _():
+            a_copy(d).start()
+
+    def before(xp):
+        return (
             jnp.where(xp >= 1, tot[0], 0.0)
             + jnp.where(xp >= 2, tot[1], 0.0)
             + jnp.where(xp >= 3, tot[2], 0.0)
         )
-        w = jnp.exp(before)[0:1]
-        for m in range(3):
+
+    def l_start(d, slots):
+        for m in slots:
+
+            @pl.when(l_used(m, (x + d) % ROW))
+            def _():
+                l_copy(m, d, x).start()
+
+    for d in (0, 1, 3, 2):
+        xp = (x + d) % ROW
+        w = jnp.exp(before(xp))[0:1]
+        for m in range(2):
             lsend[d, m] = (levels[m] * w).astype(BF16)
         near = jnp.where(xp == 1, st[0], jnp.where(xp == 2, pair, jnp.where(xp == 3, st[2], 0.0)))
         lsend[d, 3] = near.astype(BF16)
         lsend[d, 4] = (pair * jnp.exp(tot[2][0:1])).astype(BF16)
         if d > 0:
-            l_copy(0, d).start()
-
-            @pl.when(xp == 3)
-            def _():
-                l_copy(1, d).start()
+            l_start(d, (0, 1, 3, 4))
+
+    for t, d in ((1, 1), (1, 3), (0, 2), (1, 2)):
+        relay(t, d)
+
+    @pl.when(z >= 4)
+    def _():
+        pltpu.make_async_remote_copy(
+            src_ref=asend,
+            dst_ref=arecv,
+            send_sem=a_send.at[0],
+            recv_sem=a_recv.at[0],
+            device_id={"ctx": ((z + 1) % zn) * ROW + x},
+            device_id_type=MESH,
+        ).wait_recv()
+
+    whole = arecv[...].astype(F32)
+    for d in (0, 1, 3, 2):
+        w = jnp.exp(before((x + d) % ROW) + decay)[0:1]
+        lsend[d, 2] = (whole * w).astype(BF16)
+        if d > 0:
+            l_start(d, (2,))
 
     lrecv[x, 0:4] = lsend[0, 0:4]
 
@@ -506,7 +572,12 @@
 
         lax.fori_loop(0, tok // qrows, body, 0)
 
-    turns = (ROW - 1 - x, (x + 2) % ROW, x + 1 - 2 * (x % 2), x)
+    turns = (
+        jnp.where(x < 2, 3, x - 1),
+        jnp.where(x == 0, 2, jnp.where(x == 3, 1, 0)),
+        (x + 1) % ROW,
+        x,
+    )
 
     def step(k):
         j = turns[k]
@@ -536,26 +607,11 @@
     step(2)
 
     for d in range(1, ROW):
-        p = (x + ROW - d) % ROW
-        pltpu.make_async_remote_copy(
-            src_ref=lsend.at[d, pl.ds(0, 4)],
-            dst_ref=lrecv.at[p, pl.ds(0, 4)],
-            send_sem=l_send.at[0, d - 1],
-            recv_sem=l_recv.at[0, d - 1],
-            device_id={"ctx": rowdev(d)},
-            device_id_type=MESH,
-        ).wait_recv()
-
-        @pl.when(x == 3)
-        def _():
-            pltpu.make_async_remote_copy(
-                src_ref=lsend.at[d, pl.ds(4, 1)],
-                dst_ref=lrecv.at[p, pl.ds(4, 1)],
-                send_sem=l_send.at[1, d - 1],
-                recv_sem=l_recv.at[1, d - 1],
-                device_id={"ctx": rowdev(d)},
-                device_id_type=MESH,
-            ).wait_recv()
+        for m in range(5):
+
+            @pl.when(l_used(m, x))
+            def _():
+                l_copy(m, d, (x + ROW - d) % ROW).wait_recv()
 
     def across(h, acc):
         hc = cols(h)
@@ -600,11 +656,11 @@
             x_copy(t, d).wait_send()
         for c in s_copies(d):
             c.wait_send()
-        l_copy(0, d).wait_send()
-
-        @pl.when((x + d) % ROW == 3)
-        def _():
-            l_copy(1, d).wait_send()
+        for m in range(5):
+
+            @pl.when(l_used(m, (x + d) % ROW))
+            def _():
+                l_copy(m, d, x).wait_send()
 
         @pl.when(relay_if(d))
         def _():
@@ -616,12 +672,18 @@
         for t in (0, 1):
             halo_own(t).wait_send()
 
-    for d in range(1, zn):
-
-        @pl.when(z + d < zn)
+    for d in group:
+
+        @pl.when(zl + d < 4)
         def _():
             for c in r_copies(d):
                 c.wait_send()
+
+    for d in reaches:
+
+        @pl.when((z == 3) & sends_to(d))
+        def _():
+            a_copy(d).wait_send()
 
     for d in range(1, hn):
         n_copy(d).wait_send()
@@ -687,9 +749,11 @@
             vm((4, 8, 128), F32),
             vm((4, 8, 128), F32),
             vm((hd, hd), BF16),
-            vm((max(zn - 1, 1), hd, hd), BF16),
+            vm((3, hd, hd), BF16),
             vm((8, 128), F32),
-            vm((max(zn - 1, 1), 8, 128), F32),
+            vm((3, 8, 128), F32),
+            vm((hd, hd), BF16),
+            vm((hd, hd), BF16),
             vm((4, 5, hd, hd), BF16),
             vm((4, 5, hd, hd), BF16),
             vm((8, 128), F32),
@@ -701,16 +765,18 @@
             dma((2, 4)),
             dma((2, 3)),
             dma((2, 3)),
-            dma((2, max(zn - 1, 1))),
-            dma((2, max(zn - 1, 1))),
             dma((2, 3)),
             dma((2, 3)),
+            dma((5, 3)),
+            dma((5, 3)),
             dma((max(hn - 1, 1),)),
             dma((max(hn - 1, 1),)),
             dma((4,)),
             dma((4,)),
             dma((2,)),
-            pltpu.SemaphoreType.REGULAR((max(zn - 1, 1),)),
+            pltpu.SemaphoreType.REGULAR((4,)),
+            dma((4,)),
+            dma((1,)),
         ],
         compiler_params=pltpu.CompilerParams(
             collective_id=0, has_side_effects=True, vmem_limit_bytes=48 * 1024 * 1024

time: 46.3 us -> 44.4 us (0.959)
  the two profiles are of different devices: /device:TPU:131 before, /device:TPU:197 now
where the time goes in v4:
time: 44.4 us; the launch traced here: 44.3 us
  Pallas kernels  42.1 us (95%)
  local copies, waits for them, and re-layouts  1.59 us (4%)
  between operations  0.64 us (1%)
    pallas_call x1, Pallas kernels, shards(): pl.pallas_call(functools.partial(kernel, zn, hn), out_shape=(out, out), i...  42.1 us
    unnamed x2, local copies, waits for them, and re-layouts  1.59 us

profile of v4, /device:TPU:197, one launch (start us, length us, event | category | flops | bytes accessed | tf_op | source)
XLA Modules:
  0.0 44.3 jit_solution(17671676863120512362)
XLA Ops:
  0.6 42.1 %shard_map.113 = (bf16[512,512]{1,0:T(8,128)(2,1)S(1)}, bf16[512,512]{1,0:T(8,128)(2,1)S(1)}) custom-call(bf16[512,512]{1,0:T(8,128)(2,1)} %sq_hbm.1, bf16[512,512]{1,0:T(8,128)(2,1)} %sk_hbm.1, bf16[512,512]{1,0:T(8,128)(2,1)} %sv_hbm.1, bf16[512,512]{1,0:T(8,128)(2,1)} %sg_hbm.1, f32[4,512]{1,0:T(4,128)} %ld_hbm.1, f32[20,4,512]{2,1,0:T(4,128)} %bitcast.2, ...), custom_call_target="tpu_custom_call" | custom-call | flops 3000000000 | bytes 5000000 | tf_op jit(solution)/shard_map/pallas_call | solution.py:724
  42.7 0.8 %copy.14 = bf16[512,512]{1,0:T(8,128)(2,1)} copy(bf16[512,512]{1,0:T(8,128)(2,1)S(1)} %get-tuple-element.4) | data formatting | bytes 1048576
  43.5 0.8 %copy.15 = bf16[512,512]{1,0:T(8,128)(2,1)} copy(bf16[512,512]{1,0:T(8,128)(2,1)S(1)} %get-tuple-element.5) | data formatting | bytes 1048576

commit v5 on v4

--- a/solution.py
+++ b/solution.py
@@ -85,6 +85,7 @@
     o_send,
     o_recv,
     out_sem,
+    mix_sem,
     ready,
     a_send,
     a_recv,
@@ -636,6 +637,10 @@
 
     step(3)
 
+    def mix_out(i):
+        rows = pl.ds(i * chunk, chunk)
+        return pltpu.make_async_copy(mout.at[rows], mo_hbm.at[rows], mix_sem.at[i])
+
     total = nsend[...]
     for d in range(1, hn):
         n_copy(d).wait_recv()
@@ -648,8 +653,7 @@
         for h in range(ROW):
             hs = slice(h * hd, (h + 1) * hd)
             mout[rows, hs] = (gated[rows, hs] * scale_col * gainbuf[:, hs]).astype(BF16)
-    mix_out = pltpu.make_async_copy(mout, mo_hbm, out_sem.at[0])
-    mix_out.start()
+        mix_out(i).start()
 
     for d in range(1, ROW):
         for t in range(3):
@@ -705,7 +709,8 @@
         def _():
             o_local(j).wait()
 
-    mix_out.wait()
+    for i in range(chunks):
+        mix_out(i).wait()
 
 
 def hbm(*arrays):
@@ -774,6 +779,7 @@
             dma((4,)),
             dma((4,)),
             dma((2,)),
+            dma((4,)),
             pltpu.SemaphoreType.REGULAR((4,)),
             dma((4,)),
             dma((1,)),

time: 44.4 us -> 45.4 us (1.023)
  Pallas kernels: 42.1 us -> 43.1 us
    pallas_call x1, Pallas kernels: 42.1 us -> 43.1 us  [shards(): pl.pallas_call(functools.partial(kernel, zn, hn), out_shape=(out, out), i...]
where the time goes in v5:
time: 45.4 us; the launch traced here: 45.3 us
  Pallas kernels  43.1 us (95%)
  local copies, waits for them, and re-layouts  1.59 us (4%)
  between operations  0.64 us (1%)
    pallas_call x1, Pallas kernels, shards(): pl.pallas_call(functools.partial(kernel, zn, hn), out_shape=(out, out), i...  43.1 us
    unnamed x2, local copies, waits for them, and re-layouts  1.59 us

profile of v5, /device:TPU:197, one launch (start us, length us, event | category | flops | bytes accessed | tf_op | source)
XLA Modules:
  0.0 45.3 jit_solution(647193200173888412)
XLA Ops:
  0.6 43.1 %shard_map.113 = (bf16[512,512]{1,0:T(8,128)(2,1)S(1)}, bf16[512,512]{1,0:T(8,128)(2,1)S(1)}) custom-call(bf16[512,512]{1,0:T(8,128)(2,1)} %sq_hbm.1, bf16[512,512]{1,0:T(8,128)(2,1)} %sk_hbm.1, bf16[512,512]{1,0:T(8,128)(2,1)} %sv_hbm.1, bf16[512,512]{1,0:T(8,128)(2,1)} %sg_hbm.1, f32[4,512]{1,0:T(4,128)} %ld_hbm.1, f32[20,4,512]{2,1,0:T(4,128)} %bitcast.2, ...), custom_call_target="tpu_custom_call" | custom-call | flops 3000000000 | bytes 5000000 | tf_op jit(solution)/shard_map/pallas_call | solution.py:729
  43.7 0.8 %copy.14 = bf16[512,512]{1,0:T(8,128)(2,1)} copy(bf16[512,512]{1,0:T(8,128)(2,1)S(1)} %get-tuple-element.4) | data formatting | bytes 1048576
  44.5 0.8 %copy.15 = bf16[512,512]{1,0:T(8,128)(2,1)} copy(bf16[512,512]{1,0:T(8,128)(2,1)S(1)} %get-tuple-element.5) | data formatting | bytes 1048576
